TPU v7x, 256 devices: a whole 4x4x8 slice. The times are simulated.
256 devices in a mesh: pipe: 8 (over x, y_hi), ctx: 32 (over y_lo, z, core).
Axes of the slice: x: 4, y: 4 (y_hi: 2, y_lo: 2; y = y_hi * 2 + y_lo), z: 8, core: 2. Of those that a mesh axis runs over, the one named last changes fastest.
Arguments:
- queries: bfloat16 [8, 4096, 4096], P('pipe', 'ctx'), may hold values from -6 to 6
- outputs_fwd: bfloat16 [8, 4096, 4096], P('pipe', 'ctx'), may hold values from -3 to 3
- handed_grads: bfloat16 [8, 4096, 4096], P('pipe', 'ctx'), may hold values from -1.5 to 1.5
- log_norms: float32 [8, 4096, 32], P('pipe', 'ctx'), may hold values from 2 to 4
- own_keys: bfloat16 [8, 4096, 512], P('pipe', 'ctx'), may hold values from -6 to 6
- own_values: bfloat16 [8, 4096, 512], P('pipe', 'ctx'), may hold values from -6 to 6
- pool_keys: bfloat16 [8, 2048, 512], P('pipe', 'ctx'), may hold values from -6 to 6
- pool_values: bfloat16 [8, 2048, 512], P('pipe', 'ctx'), may hold values from -6 to 6
- block_tables: int32 [8, 64, 32], P('pipe', 'ctx'), may hold values from -1 to 63, as said below
- lengths: int32 [8, 64], P('pipe', 'ctx'), may hold values from 1 to 64, 3072 in all within a row
Outputs:
- grad_queries: bfloat16 [8, 4096, 4096], P('pipe', 'ctx')
- grad_own_keys: bfloat16 [8, 4096, 512], P('pipe', 'ctx')
- grad_own_values: bfloat16 [8, 4096, 512], P('pipe', 'ctx')
- grad_pool_keys: float32 [8, 2048, 512], P('pipe', 'ctx')
- grad_pool_values: float32 [8, 2048, 512], P('pipe', 'ctx')
Inputs may be any that keep to these rules, and one draw needn't show every extreme that they name: `block_tables`: each response lists prompt block numbers in its first 1 to 32 entries (repeats allowed) and -1 in the rest; in every section some response uses all 32 entries. `lengths`: in every section the longest response has exactly 64 tokens.
All inputs are finite; a program needn't handle non-finite values. No bound on the sum of `lengths` on one device may be relied on, other than what follows from the above.
Results may differ from a plain program's by a relative error of at most 0.0063.
Values may be sent and summed in bfloat16 or wider, within the bound.
A program may use at most 128 MiB of HBM per device.

v0:
```python
import math

import jax
import jax.numpy as jnp
from jax import lax
from jax.sharding import PartitionSpec as P

HQ = 32
KVH = 4
HD = 128
BLK = 32
RLEN = 64


def shifted(value, axis, steps):
    count = lax.axis_size(axis)
    pairs = [(source, (source + steps) % count) for source in range(count)]
    return lax.ppermute(value, axis, pairs)


def split_heads(matrix):
    row_count = matrix.shape[0]
    return matrix.reshape(row_count, KVH, HQ // KVH, HD).transpose(1, 2, 0, 3)


def merge_heads(grad_heads):
    row_count = grad_heads.shape[2]
    return grad_heads.transpose(2, 0, 1, 3).reshape(row_count, HQ * HD)


def head_inputs(queries, fwd_out, cotangent, log_norms):
    row_count = queries.shape[0]
    products = cotangent.astype(jnp.float32) * fwd_out.astype(jnp.float32)
    row_dots = jnp.sum(products.reshape(row_count, HQ, HD), axis=-1)
    norm_heads = log_norms.reshape(row_count, KVH, HQ // KVH).transpose(1, 2, 0)
    dot_heads = row_dots.reshape(row_count, KVH, HQ // KVH).transpose(1, 2, 0)
    return (split_heads(queries), split_heads(cotangent), norm_heads, dot_heads)


def key_terms(head_data, key_rows, value_rows, visible):
    query_heads, grad_heads, norm_heads, dot_heads = head_data
    score_scale = HD ** (-0.5)
    key_count = key_rows.shape[0]
    key_heads = key_rows.reshape(key_count, KVH, HD).transpose(1, 0, 2)
    value_heads = value_rows.reshape(key_count, KVH, HD).transpose(1, 0, 2)
    scores = (
        jnp.einsum("hgrd,hnd->hgrn", query_heads, key_heads, preferred_element_type=jnp.float32)
        * score_scale
    )
    probs = jnp.where(visible[None, None], jnp.exp(scores - norm_heads[..., None]), 0.0)
    dprobs = jnp.einsum(
        "hgrd,hnd->hgrn", grad_heads, value_heads, preferred_element_type=jnp.float32
    )
    dscores_low = (probs * (dprobs - dot_heads[..., None])).astype(jnp.bfloat16)
    grad_query = None
    grad_pair = None
    grad_query = (
        jnp.einsum("hgrn,hnd->hgrd", dscores_low, key_heads, preferred_element_type=jnp.float32)
        * score_scale
    )
    probs_low = probs.astype(jnp.bfloat16)
    grad_key = (
        jnp.einsum("hgrn,hgrd->hnd", dscores_low, query_heads, preferred_element_type=jnp.float32)
        * score_scale
    )
    grad_value = jnp.einsum(
        "hgrn,hgrd->hnd", probs_low, grad_heads, preferred_element_type=jnp.float32
    )
    grad_pair = jnp.concatenate(
        [
            grad_key.transpose(1, 0, 2).reshape(key_count, KVH * HD),
            grad_value.transpose(1, 0, 2).reshape(key_count, KVH * HD),
        ],
        axis=1,
    )
    return (grad_query, grad_pair)


def key_sweep(head_data, key_rows, value_rows, visible_fn, first_row):
    key_count = key_rows.shape[0]
    block_size = math.gcd(key_count, 256)
    block_total = key_count // block_size

    def one_block(running, block_index):
        offset = block_index * block_size
        block_keys = lax.dynamic_slice_in_dim(key_rows, offset, block_size, 0)
        block_values = lax.dynamic_slice_in_dim(value_rows, offset, block_size, 0)
        visible = visible_fn(first_row + offset, block_size)
        grad_query, grad_pair = key_terms(head_data, block_keys, block_values, visible)
        running = running + grad_query
        return (running, grad_pair)

    start_sum = jnp.zeros(head_data[0].shape, jnp.float32)
    running, grad_pairs = lax.scan(one_block, start_sum, jnp.arange(block_total, dtype=jnp.int32))
    grad_pairs = grad_pairs.reshape(key_count, 2 * KVH * HD)
    return (running, grad_pairs)


def local(
    queries,
    outputs_fwd,
    handed_grads,
    log_norms,
    own_keys,
    own_values,
    pool_keys,
    pool_values,
    block_tables,
    lengths,
):
    cotangent = shifted(handed_grads, "pipe", -1)
    head_data = head_inputs(queries[0], outputs_fwd[0], cotangent[0], log_norms[0])
    row_count = queries.shape[1]
    tables = block_tables[0]
    resp_lengths = lengths[0]
    position = jnp.arange(RLEN, dtype=jnp.int32)
    live_rows = position[None, :] < resp_lengths[:, None]
    live_flat = live_rows.reshape(row_count)
    key_width = KVH * HD

    def pool_visible(first_row, span_len):
        block_ids = (first_row + jnp.arange(span_len, dtype=jnp.int32)) // BLK
        listed = jnp.any(tables[:, :, None] == block_ids[None, None, :], axis=1)
        return (listed[:, None, :] & live_rows[:, :, None]).reshape(row_count, span_len)

    def own_visible(first_row, span_len):
        key_idx = first_row + jnp.arange(span_len, dtype=jnp.int32)
        query_idx = jnp.arange(row_count, dtype=jnp.int32)
        same_resp = (query_idx // RLEN)[:, None] == (key_idx // RLEN)[None, :]
        causal = (key_idx % RLEN)[None, :] <= (query_idx % RLEN)[:, None]
        return same_resp & causal & live_flat[:, None]

    own_q, own_pair = key_sweep(head_data, own_keys[0], own_values[0], own_visible, 0)
    piece_keys = lax.all_gather(pool_keys, "ctx", axis=1, tiled=True)
    piece_values = lax.all_gather(pool_values, "ctx", axis=1, tiled=True)
    grad_query, grad_pair = key_sweep(
        head_data, piece_keys[0], piece_values[0], pool_visible, jnp.int32(0)
    )
    partial_kv = grad_pair
    pool_q, partial_kv = (grad_query, partial_kv)
    summed = lax.psum_scatter(partial_kv, "ctx", scatter_dimension=0, tiled=True)
    grad_queries = merge_heads(pool_q + own_q).astype(jnp.bfloat16)[None]
    grad_own_keys = own_pair[:, :key_width].astype(jnp.bfloat16)[None]
    grad_own_values = own_pair[:, key_width:].astype(jnp.bfloat16)[None]
    return (
        grad_queries,
        grad_own_keys,
        grad_own_values,
        summed[:, :key_width][None],
        summed[:, key_width:][None],
    )


def solution(mesh):
    in_specs = (
        P("pipe", "ctx", None),
        P("pipe", "ctx", None),
        P("pipe", "ctx", None),
        P("pipe", "ctx", None),
        P("pipe", "ctx", None),
        P("pipe", "ctx", None),
        P("pipe", "ctx", None),
        P("pipe", "ctx", None),
        P("pipe", "ctx", None),
        P("pipe", "ctx"),
    )
    out_specs = (
        P("pipe", "ctx", None),
        P("pipe", "ctx", None),
        P("pipe", "ctx", None),
        P("pipe", "ctx", None),
        P("pipe", "ctx", None),
    )
    return jax.shard_map(local, mesh=mesh, in_specs=in_specs, out_specs=out_specs, check_vma=False)
```

profile of v0, /device:TPU:1, one launch (start us, length us, event | category | flops | bytes accessed | tf_op | source)
XLA Modules:
  0.0 441.2 jit_solution(14812730467330118684)
XLA Ops:
  8.7 2.3 copy.92
  11.1 6.0 %collective-permute-start = (bf16[1,128,4096]{1,2,0:T(8,128)(2,1)}, bf16[1,128,4096]{1,2,0:T(8,128)(2,1)}, u32[]{:S(2)}, u32[]{:S(2)}) collective-permute-start(bf16[1,128,4096]{1,2,0:T(8,128)(2,1)} %copy.92), channel_id=1, source_target_pairs={{0,224},{32,0},{64,32},{96,64},{128,96},{160,128},{192,160},{224,1... | collective-permute-start | bytes 3145736 | tf_op jit(solution)/shard_map/ppermute | solution.py:18
  17.7 1.4 copy.94
  19.1 20.2 %collective-permute-done = bf16[1,128,4096]{1,2,0:T(8,128)(2,1)} collective-permute-done((bf16[1,128,4096]{1,2,0:T(8,128)(2,1)}, bf16[1,128,4096]{1,2,0:T(8,128)(2,1)}, u32[]{:S(2)}, u32[]{:S(2)}) %collective-permute-start) | collective-permute-done | bytes 1048608 | tf_op jit(solution)/shard_map/ppermute | solution.py:18
  39.3 1.7 convert_multiply_fusion
  41.2 51.3 %all-gather.3.cloned.1.call-done = bf16[1,2048,512]{2,1,0:T(8,128)(2,1)} async-done(((bf16[1,64,512]{2,1,0:T(8,128)(2,1)}), bf16[1,2048,512]{2,1,0:T(8,128)(2,1)}) %all-gather.3.cloned.1.call-update) | async-done | bytes 2097168 | tf_op jit(solution)/shard_map/all_gather | solution.py:134
  92.5 63.6 %all-gather.5.cloned.1.call-done = bf16[1,2048,512]{2,1,0:T(8,128)(2,1)} async-done(((bf16[1,64,512]{2,1,0:T(8,128)(2,1)}), bf16[1,2048,512]{2,1,0:T(8,128)(2,1)}) %all-gather.5.cloned.1.call-update) | async-done | bytes 2097168 | tf_op jit(solution)/shard_map/all_gather | solution.py:135
  156.1 152.5 %while.20 = (s32[]{:T(128)}, f32[4,8,128,128]{3,2,1,0:T(8,128)}, f32[8,256,1024]{2,1,0:T(8,128)}, s32[1,2,32]{2,1,0:T(2,128)S(1)}, s32[8]{0:T(128)S(1)}, /*index...) while((s32[]{:T(128)}, f32[4,8,128,128]{3,2,1,0:T(8,128)}, ...), condition=%wide.region_3.4_spmd.clone, body=%wide.region_1.3_spmd.clone.sunk | while | flops 1354698368 | bytes 55529488 | solution.py:94
  157.3 1.1 constant_dynamic-slice_fusion.3
  158.7 2.7 fusion.63
  162.9 3.9 fusion.64
  166.8 2.3 select_add_fusion.2
  169.7 2.2 fusion.65
  173.1 1.1 constant_dynamic-update-slice_fusion.2
  175.4 1.1 constant_dynamic-slice_fusion.3
  176.8 2.7 fusion.63
  180.9 3.9 fusion.64
  184.8 4.0 select_add_fusion.2
  188.9 2.2 fusion.65
  192.3 1.1 constant_dynamic-update-slice_fusion.2
  194.6 1.1 constant_dynamic-slice_fusion.3
  196.0 2.7 fusion.63
  200.1 3.9 fusion.64
  204.0 4.0 select_add_fusion.2
  208.1 2.2 fusion.65
  211.5 1.0 constant_dynamic-update-slice_fusion.2
  213.8 1.1 constant_dynamic-slice_fusion.3
  215.2 2.7 fusion.63
  219.3 3.9 fusion.64
  223.2 4.0 select_add_fusion.2
  227.2 2.2 fusion.65
  230.6 1.1 constant_dynamic-update-slice_fusion.2
  232.9 1.1 constant_dynamic-slice_fusion.3
  234.3 2.7 fusion.63
  238.5 3.9 fusion.64
  242.4 4.0 select_add_fusion.2
  246.4 2.2 fusion.65
  249.8 1.1 constant_dynamic-update-slice_fusion.2
  252.1 1.1 constant_dynamic-slice_fusion.3
  253.5 2.7 fusion.63
  257.7 3.9 fusion.64
  261.6 4.0 select_add_fusion.2
  265.6 2.2 fusion.65
  269.0 1.1 constant_dynamic-update-slice_fusion.2
  271.3 1.1 constant_dynamic-slice_fusion.3
  272.7 2.7 fusion.63
  276.9 3.9 fusion.64
  280.8 4.0 select_add_fusion.2
  284.8 2.2 fusion.65
  288.2 1.1 constant_dynamic-update-slice_fusion.2
  290.6 1.1 constant_dynamic-slice_fusion.3
  291.9 2.7 fusion.63
  296.1 3.9 fusion.64
  300.0 4.0 select_add_fusion.2
  304.0 2.2 fusion.65
  307.5 1.1 constant_dynamic-update-slice_fusion.2
  308.6 0.9 copy-done.4
  309.9 2.0 exponential_select_fusion
  311.9 1.6 copy.93
  313.5 2.0 multiply_convert_fusion
  316.8 2.3 fusion.19
  321.8 1.3 copy.106
  323.1 109.9 %reduce-scatter.2.cloned.1.call-done = f32[64,1024]{1,0:T(8,128)} async-done(((f32[2048,1024]{1,0:T(8,128)}), f32[64,1024]{1,0:T(8,128)}) %reduce-scatter.2.cloned.1.call-update) | async-done | bytes 262160 | tf_op jit(solution)/shard_map/reduce_scatter | solution.py:141
  433.0 1.7 slice_bitcast_fusion
  (166 shorter events, 35.6 us)
Async XLA Ops:
  7.2 9.9 %copy-start.2 = (bf16[1,128,4096]{2,1,0:T(8,128)(2,1)S(1)}, bf16[1,128,4096]{2,1,0:T(8,128)(2,1)}, u32[]{:S(2)}) copy-start(bf16[1,128,4096]{2,1,0:T(8,128)(2,1)} %param.12) | copy-start | bytes 3145732
  7.2 85.3 %all-gather.3.cloned.1.call-start = ((), (), s32[]{:S(2)}) async-start(), calls=%async_computation.1 | async-start | bytes 2162688 | tf_op jit(solution)/shard_map/all_gather | solution.py:134
  7.9 148.2 %all-gather.5.cloned.1.call-start = ((), (), s32[]{:S(2)}) async-start(), calls=%async_computation.2 | async-start | bytes 2162688 | tf_op jit(solution)/shard_map/all_gather | solution.py:135
  8.7 9.0 %copy-start.3 = (bf16[1,128,4096]{2,1,0:T(8,128)(2,1)S(1)}, bf16[1,128,4096]{2,1,0:T(8,128)(2,1)}, u32[]{:S(2)}) copy-start(bf16[1,128,4096]{2,1,0:T(8,128)(2,1)} %param.13) | copy-start | bytes 3145732
  8.7 424.3 %reduce-scatter.2.cloned.1.call-start = ((), (), s32[]{:S(2)}) async-start(), calls=%async_computation.3 | async-start | bytes 8650752 | tf_op jit(solution)/shard_map/reduce_scatter | solution.py:141
  11.1 28.2 %collective-permute-start = (bf16[1,128,4096]{1,2,0:T(8,128)(2,1)}, bf16[1,128,4096]{1,2,0:T(8,128)(2,1)}, u32[]{:S(2)}, u32[]{:S(2)}) collective-permute-start(bf16[1,128,4096]{1,2,0:T(8,128)(2,1)} %copy.92), channel_id=1, source_target_pairs={{0,224},{32,0},{64,32},{96,64},{128,96},{160,128},{192,160},{224,1... | collective-permute-start | bytes 3145736 | tf_op jit(solution)/shard_map/ppermute | solution.py:18
  41.0 115.1 %copy-start.6 = (s32[1,2,32]{2,1,0:T(2,128)S(1)}, s32[1,2,32]{2,1,0:T(2,128)}, u32[]{:S(2)}) copy-start(s32[1,2,32]{2,1,0:T(2,128)} %param.20) | copy-start | bytes 772
  41.0 115.1 %copy-start.7 = (f32[1,128,32]{1,2,0:T(8,128)S(1)}, f32[1,128,32]{1,2,0:T(8,128)}, u32[]{:S(2)}) copy-start(f32[1,128,32]{1,2,0:T(8,128)} %param.15) | copy-start | bytes 49156
  41.0 115.1 %copy-start.8 = (s32[1,2]{1,0:T(1,128)S(1)}, s32[1,2]{1,0:T(1,128)}, u32[]{:S(2)}) copy-start(s32[1,2]{1,0:T(1,128)} %param.21) | copy-start | bytes 28
  166.8 2.9 copy-start
  184.8 4.0 copy-start
  204.0 4.0 copy-start
  223.2 4.0 copy-start
  242.4 4.0 copy-start
  261.6 4.0 copy-start
  280.8 4.0 copy-start
  300.0 4.0 copy-start
  308.5 0.9 copy-start.4
  308.5 1.2 copy-start.5
  319.1 1.7 copy-start.1
Sparse Core Ops, SparseCore 0:
  9.9 82.5 all-gather.2
  94.4 61.6 all-gather.4
  308.7 124.2 reduce-scatter.1
where the time goes:
time: 446 us; the launch traced here: 441 us
  waiting for transfers between devices  246 us (55%)
  matrix products  114 us (26%)
  local copies, waits for them, and re-layouts  49.7 us (11%)
  between operations  13.9 us (3%)
  starting transfers between devices  6.08 us (1%)
  loops' own time  6.03 us (1%)
  other arithmetic  5.12 us (1%)
    reduce_scatter x1, waiting for transfers between devices, local(): lax.psum_scatter(partial_kv, 'ctx', scatter_dimension=0, tiled=True)  110 us
    all_gather x1, waiting for transfers between devices, local(): piece_values = lax.all_gather(pool_values, 'ctx', axis=1, tiled=True)  63.6 us
    all_gather x1, waiting for transfers between devices, local(): piece_keys = lax.all_gather(pool_keys, 'ctx', axis=1, tiled=True)  51.3 us
    dot_general x9, matrix products, key_terms(): jnp.einsum('hgrd,hnd->hgrn', grad_heads, value_heads, preferred_element_t...  33.2 us
    dot_general x9, matrix products, key_terms(): jnp.einsum('hgrn,hnd->hgrd', dscores_low, key_heads, preferred_element_ty...  30.9 us
    dot_general x9, matrix products, key_terms(): jnp.einsum('hgrd,hnd->hgrn', query_heads, key_heads, preferred_element_ty...  23.3 us
    ppermute x1, waiting for transfers between devices, shifted(): return lax.ppermute(value, axis, pairs)  20.2 us
    dot_general x9, matrix products, key_terms(): jnp.einsum('hgrn,hgrd->hnd', probs_low, grad_heads, preferred_element_typ...  19.7 us
  transfers between devices with their start and end apart: 4, of which 4 were waited for; matrix products, arithmetic and copies ran while one was open for 4% of the time, Pallas kernels for 0%

commit v1 on v0

v1 whole, which is shorter than its diff:
```python
import functools
import math

import jax
import jax.numpy as jnp
from jax import lax
from jax.experimental import pallas as pl
from jax.experimental.pallas import tpu as pltpu
from jax.sharding import PartitionSpec as P

HD = 128
ROWS = 128
RLEN = 64
BLK = 32
GROUP = 8
SCALE = HD ** -0.5
EXP_SCALE = SCALE * math.log2(math.e)
FAR = 1e30
BF = jnp.bfloat16
F32 = jnp.float32
MESH = pl.DeviceIdType.MESH


def split3(x):
    hi = x.astype(BF).astype(F32)
    rest = x - hi
    mid = rest.astype(BF).astype(F32)
    return hi, mid, rest - mid


def dot(a, b):
    return jnp.dot(a, b, preferred_element_type=F32)


def kernel(
    zs, pipes,
    q_hbm, o_hbm, g_hbm, ln_ref, ok_hbm, ov_hbm, pk_hbm, pv_hbm, tab_ref, len_ref,
    dq_out, dok_out, dov_out, dpk_out, dpv_out,
    qb, ob, cb, qh, ch, qt, ct, kv, kaug, okv, dqt, ds_s, p_s,
    send_buf, recv_buf, fin, fsend, frecv, dq_st, ok_st, ln_t, ln_r, bp_s, bp,
    loc_sem, sib_send, sib_recv, cot_send, cot_recv, kv_send, kv_recv,
    ga_send, ga_recv, rs_send, rs_recv, f_send, f_recv, out_sem, out_send, out_recv,
):
    p = lax.axis_index("pipe")
    c = lax.axis_index("ctx")
    core = lax.rem(c, 2)
    z = lax.rem(lax.div(c, 2), zs)
    yl = lax.div(c, 2 * zs)
    oc = 1 - core

    def dev(pp, yy, zz, kk):
        return (pp, (yy * zs + zz) * 2 + kk)

    sib = dev(p, yl, z, oc)
    z_up = lax.rem(z + 1, zs)
    z_dn = lax.rem(z + zs - 1, zs)
    p_up = lax.rem(p + 1, pipes)
    p_dn = lax.rem(p + pipes - 1, pipes)
    ring_dst = (dev(p, yl, z_up, core), dev(p, yl, z_dn, core))

    def half(ref, kk, width):
        return ref.at[:, pl.ds(pl.multiple_of(kk * width, 128), width)]

    def remote(src, dst, ss, rs, to):
        return pltpu.make_async_remote_copy(
            src_ref=src, dst_ref=dst, send_sem=ss, recv_sem=rs, device_id=to, device_id_type=MESH
        )

    my_rows = pl.ds(pl.multiple_of(core * ROWS, ROWS), ROWS)
    my_half = pl.ds(pl.multiple_of(core * 64, 64), 64)
    my_chunk = yl * zs + z

    loc = [
        pltpu.make_async_copy(half(q_hbm, core, 2048), qb.at[my_rows], loc_sem.at[0]),
        pltpu.make_async_copy(half(o_hbm, core, 2048), ob.at[my_rows], loc_sem.at[1]),
        pltpu.make_async_copy(half(ok_hbm, core, 256), okv.at[my_rows, 0:256], loc_sem.at[2]),
        pltpu.make_async_copy(half(ov_hbm, core, 256), okv.at[my_rows, 256:512], loc_sem.at[3]),
        pltpu.make_async_copy(half(pk_hbm, core, 256), kv.at[my_chunk, my_half, 0:256], loc_sem.at[4]),
        pltpu.make_async_copy(half(pv_hbm, core, 256), kv.at[my_chunk, my_half, 256:512], loc_sem.at[5]),
    ]
    for cp in loc:
        cp.start()

    row = lax.broadcasted_iota(jnp.int32, (ROWS, 32), 0)
    length = jnp.where(row < RLEN, len_ref[0, 0], len_ref[0, 1])
    live = lax.rem(row, RLEN) < length
    ln_t[...] = jnp.where(live, ln_ref[...] * (1.0 / SCALE), FAR).T
    lane = lax.broadcasted_iota(jnp.int32, bp_s.shape, 1)
    ids = lax.broadcasted_iota(jnp.int32, (bp_s.shape[0], tab_ref.shape[1]), 0)
    offs = jnp.zeros(bp_s.shape, F32)
    for rr in range(2):
        hit = jnp.where(tab_ref[rr : rr + 1, :] == ids, 1.0, 0.0)
        listed = jnp.max(hit, axis=1, keepdims=True)
        offs = jnp.where(lane == 3 + 2 * core + rr, (listed - 1.0) * FAR, offs)
    bp_s[...] = offs
    bp[core] = offs
    ln_r[core] = ln_t[pl.ds(pl.multiple_of(core * 16, 16), 16), :]

    barrier = pltpu.get_barrier_semaphore()
    partners = [
        sib,
        dev(p, 1 - yl, z, 0), dev(p, 1 - yl, z, 1),
        ring_dst[0], ring_dst[1],
        dev(p_dn, yl, z, 0), dev(p_dn, yl, z, 1),
        dev(p_up, yl, z, 0), dev(p_up, yl, z, 1),
    ]
    for to in partners:
        pl.semaphore_signal(barrier, inc=1, device_id=to, device_id_type=MESH)
    pl.semaphore_wait(barrier, len(partners))

    group = [(yl, oc), (1 - yl, core), (1 - yl, oc)]
    kv_out = []
    for i, (yy, kk) in enumerate(group):
        for j, src in enumerate((pk_hbm, pv_hbm)):
            kv_out.append(
                remote(
                    half(src, kk, 256),
                    kv.at[my_chunk, my_half, j * 256 : (j + 1) * 256],
                    kv_send.at[i, j], kv_recv.at[i, j], dev(p, yy, z, kk),
                )
            )
    for cp in kv_out:
        cp.start()

    cot_out = []
    for j in range(2):
        for d in range(2):
            kk = jnp.where(d == 0, oc, core)
            cot_out.append(
                remote(
                    g_hbm.at[:, pl.ds(pl.multiple_of(kk * 2048 + j * 1024, 128), 1024)],
                    cb.at[my_rows, j * 1024 : (j + 1) * 1024],
                    cot_send.at[j, d], cot_recv.at[j, d], dev(p_dn, yl, z, kk),
                )
            )
    for cp in cot_out:
        cp.start()

    sib_out = [
        remote(half(q_hbm, oc, 2048), qb.at[my_rows], sib_send.at[0], sib_recv.at[0], sib),
        remote(half(o_hbm, oc, 2048), ob.at[my_rows], sib_send.at[1], sib_recv.at[1], sib),
        remote(half(ok_hbm, oc, 256), okv.at[my_rows, 0:256], sib_send.at[2], sib_recv.at[2], sib),
        remote(half(ov_hbm, oc, 256), okv.at[my_rows, 256:512], sib_send.at[3], sib_recv.at[3], sib),
        remote(ln_t.at[pl.ds(pl.multiple_of(oc * 16, 16), 16)], ln_r.at[core], sib_send.at[4], sib_recv.at[4], sib),
        remote(bp_s, bp.at[core], sib_send.at[5], sib_recv.at[5], sib),
    ]
    for cp in sib_out:
        cp.start()

    def chunk_id(d, t):
        return lax.rem(z + zs - t, zs) if d == 0 else zs + lax.rem(z + t, zs)

    def gather(d, t):
        ref = kv.at[chunk_id(d, t)]
        return remote(ref, ref, ga_send.at[d, t], ga_recv.at[d, t], ring_dst[d])

    def gather_wait(d, t):
        ref = kv.at[chunk_id(d, t + 1)]
        remote(ref, ref, ga_send.at[d, t], ga_recv.at[d, t], ring_dst[d]).wait_recv()

    loc[4].wait()
    loc[5].wait()
    for cp in kv_out:
        cp.wait_recv()
    for d in range(2):
        gather(d, 0).start()

    qt[:, 128:256, :] = jnp.zeros((2, 128, 2048), BF)
    ct[:, 128:256, :] = jnp.zeros((2, 128, 2048), BF)
    recv_buf[:, 0] = jnp.zeros(recv_buf.shape[:1] + recv_buf.shape[2:], BF)
    loc[0].wait()
    sib_out[0].wait_recv()
    sib_out[4].wait_recv()
    sub = lax.broadcasted_iota(jnp.int32, (16, 128), 0)
    col = lax.broadcasted_iota(jnp.int32, (16, 128), 1)

    def tile_cols(side, g):
        return slice(side * 1024 + g * 128, side * 1024 + (g + 1) * 128)

    def query_tiles(h, side):
        for g in range(GROUP):
            cols = tile_cols(side, g)
            tile = qb[side * 128 : (side + 1) * 128, (h * 8 + g) * 128 : (h * 8 + g + 1) * 128]
            qh[h, cols, :] = tile
            qt[h, 0:128, cols] = tile.T
            hi, mid, low = split3(ln_r[side, h * 8 + g : h * 8 + g + 1, :])
            own = jnp.where(sub - 3 == side * 2 + lax.div(col, RLEN), 1.0, 0.0)
            aug = jnp.where(sub == 0, -hi, jnp.where(sub == 1, -mid, jnp.where(sub == 2, -low, own)))
            qt[h, 128:144, cols] = aug.astype(BF)

    def cot_tiles(h, side):
        for g in range(GROUP):
            cols = tile_cols(side, g)
            rows, lanes = slice(side * 128, (side + 1) * 128), slice((h * 8 + g) * 128, (h * 8 + g + 1) * 128)
            tile = cb[rows, lanes]
            ch[h, cols, :] = tile
            tile_t = tile.T
            ct[h, 0:128, cols] = tile_t
            prod = tile_t.astype(F32) * ob[rows, lanes].T.astype(F32)
            hi, mid, low = split3(jnp.sum(prod, axis=0, keepdims=True))
            aug = jnp.where(sub == 0, hi, jnp.where(sub == 1, mid, jnp.where(sub == 2, low, 0.0)))
            ct[h, 128:144, cols] = aug.astype(BF)

    for h in range(2):
        for side in range(2):
            query_tiles(h, side)

    def gather_step(t, carry):
        for d in range(2):
            gather_wait(d, t - 1)
            gather(d, t).start()
        return carry

    lax.fori_loop(1, zs - 1, gather_step, 0)

    sib_out[5].wait_recv()
    aug_lane = lax.broadcasted_iota(jnp.int32, bp_s.shape, 1)
    blocks = bp[0] + bp[1] + jnp.where(aug_lane < 3, 1.0, 0.0)
    spread = jnp.broadcast_to(blocks[:, None, :], (blocks.shape[0], BLK, 128))
    kaug[...] = spread.reshape(kaug.shape).astype(BF)

    loc[1].wait()
    sib_out[1].wait_recv()
    for cp in cot_out:
        cp.wait_recv()
    for h in range(2):
        for side in range(2):
            cot_tiles(h, side)

    for i in (2, 3):
        loc[i].wait()
        sib_out[i].wait_recv()
    one_lane = lax.broadcasted_iota(jnp.int32, (256, 128), 1) < 3
    v_cst = jnp.where(one_lane, -1.0, 0.0).astype(BF)
    k_cst = jnp.where(one_lane, 1.0, 0.0).astype(BF)
    key_i = lax.broadcasted_iota(jnp.int32, (ROWS, 1024), 0)
    row_i = lax.rem(lax.broadcasted_iota(jnp.int32, (ROWS, 1024), 1), ROWS)
    seen = (lax.div(key_i, RLEN) == lax.div(row_i, RLEN)) & (key_i <= row_i)
    for h in range(2):
        for side in range(2):
            rows = slice(side * 128, (side + 1) * 128)
            cols = slice(side * 1024, (side + 1) * 1024)
            k_l = okv[rows, h * 128 : (h + 1) * 128]
            v_l = okv[rows, 256 + h * 128 : 256 + (h + 1) * 128]
            s = dot(jnp.concatenate([k_l, k_cst[:128]], 1), qt[h, :, cols])
            pr = jnp.where(seen, jnp.exp2(s * EXP_SCALE), 0.0)
            dp = dot(jnp.concatenate([v_l, v_cst[:128]], 1), ct[h, :, cols])
            ds = (pr * dp).astype(BF)
            dqt[h, :, cols] = dot(k_l.T, ds)
            ok_st[side, :, h * 128 : (h + 1) * 128] = (dot(ds, qh[h, cols, :]) * SCALE).astype(BF)
            ok_st[side, :, 256 + h * 128 : 256 + (h + 1) * 128] = dot(pr.astype(BF), ch[h, cols, :]).astype(BF)

    for d in range(2):
        gather_wait(d, zs - 2)

    ok_out = []
    for j, out in enumerate((dok_out, dov_out)):
        lanes = slice(j * 256, (j + 1) * 256)
        ok_out.append(remote(ok_st.at[oc, :, lanes], half(out, core, 256), out_send.at[j], out_recv.at[j], sib))
        ok_out.append(pltpu.make_async_copy(ok_st.at[core, :, lanes], half(out, core, 256), out_sem.at[j]))
    for cp in ok_out:
        cp.start()

    def rs_copy(d, s):
        return remote(
            send_buf.at[d, s], recv_buf.at[d, s + 1], rs_send.at[d, s], rs_recv.at[d, s], ring_dst[d]
        )

    def step(s, carry):
        ids = [chunk_id(d, lax.rem(s + 1, zs)) for d in range(2)]
        k_aug = jnp.concatenate([kaug[ids[0]], kaug[ids[1]]], 0)
        for h in range(2):
            lanes = slice(h * 128, (h + 1) * 128)
            v_lanes = slice(256 + h * 128, 256 + (h + 1) * 128)
            k_l = jnp.concatenate([kv[ids[0], :, lanes], kv[ids[1], :, lanes]], 0)
            v_l = jnp.concatenate([kv[ids[0], :, v_lanes], kv[ids[1], :, v_lanes]], 0)
            k_full = jnp.concatenate([k_l, k_aug], 1)
            v_full = jnp.concatenate([v_l, v_cst], 1)
            k_t = k_l.T
            for n in range(4):
                cols = slice(n * 512, (n + 1) * 512)
                pr = jnp.exp2(dot(k_full, qt[h, :, cols]) * EXP_SCALE)
                dp = dot(v_full, ct[h, :, cols])
                ds = (pr * dp).astype(BF)
                p_s[:, cols] = pr.astype(BF)
                ds_s[:, cols] = ds
                dqt[h, :, cols] += dot(k_t, ds)
            dk = dot(ds_s[...], qh[h])
            dv = dot(p_s[...], ch[h])
            for d in range(2):
                fin[d, :, lanes] = dk[d * 128 : (d + 1) * 128]
                fin[d, :, v_lanes] = dv[d * 128 : (d + 1) * 128]

        @pl.when(s > 0)
        def _():
            for d in range(2):
                rs_copy(d, s - 1).wait_recv()

        for d in range(2):
            fin[d] = fin[d] + recv_buf[d, s].astype(F32)

        @pl.when(s < zs - 1)
        def _():
            for d in range(2):
                send_buf[d, s] = fin[d].astype(BF)
                rs_copy(d, s).start()

        return carry

    lax.fori_loop(0, zs, step, 0)

    fsend[...] = fin[...].astype(BF)
    me4 = yl * 2 + core
    f_out = [
        remote(
            fsend.at[yy, pl.ds(pl.multiple_of(kk * 64, 64), 64)],
            frecv.at[me4], f_send.at[i], f_recv.at[i], dev(p, yy, z, kk),
        )
        for i, (yy, kk) in enumerate(group)
    ]
    for cp in f_out:
        cp.start()
    frecv[me4] = fsend[yl, my_half, :]

    for h in range(2):
        for side in range(2):
            for g in range(GROUP):
                tile = dqt[h, :, tile_cols(side, g)] * SCALE
                dq_st[side, :, (h * 8 + g) * 128 : (h * 8 + g + 1) * 128] = tile.T.astype(BF)
    dq_copies = [
        remote(dq_st.at[oc], half(dq_out, core, 2048), out_send.at[2], out_recv.at[2], sib),
        pltpu.make_async_copy(dq_st.at[core], half(dq_out, core, 2048), out_sem.at[2]),
    ]
    for cp in dq_copies:
        cp.start()

    for cp in f_out:
        cp.wait_recv()
    for kk in range(2):
        tot = frecv[kk].astype(F32) + frecv[2 + kk].astype(F32)
        dpk_out[:, kk * 256 : (kk + 1) * 256] = tot[:, 0:256] * SCALE
        dpv_out[:, kk * 256 : (kk + 1) * 256] = tot[:, 256:512]

    for cp in ok_out + dq_copies:
        cp.wait()
    for cp in kv_out + cot_out + sib_out + f_out:
        cp.wait_send()

    def drain(t, carry):
        for d in range(2):
            gather(d, t).wait_send()
            rs_copy(d, t).wait_send()
        return carry

    lax.fori_loop(0, zs - 1, drain, 0)


def local(zs, pipes, q, o, g, ln, ok, ov, pk, pv, tab, lens):
    any_ = pl.BlockSpec(memory_space=pl.ANY)
    vmem = pl.BlockSpec(memory_space=pltpu.VMEM)
    smem = pl.BlockSpec(memory_space=pltpu.SMEM)
    chunks = 2 * zs
    blocks = chunks * 128 // BLK
    dma = pltpu.SemaphoreType.DMA
    outs = pl.pallas_call(
        functools.partial(kernel, zs, pipes),
        out_shape=(
            jax.ShapeDtypeStruct((ROWS, 4096), BF),
            jax.ShapeDtypeStruct((ROWS, 512), BF),
            jax.ShapeDtypeStruct((ROWS, 512), BF),
            jax.ShapeDtypeStruct((64, 512), F32),
            jax.ShapeDtypeStruct((64, 512), F32),
        ),
        in_specs=[any_, any_, any_, vmem, any_, any_, any_, any_, vmem, smem],
        out_specs=(any_, any_, any_, vmem, vmem),
        scratch_shapes=[
            pltpu.VMEM((256, 2048), BF),
            pltpu.VMEM((256, 2048), BF),
            pltpu.VMEM((256, 2048), BF),
            pltpu.VMEM((2, 2048, 128), BF),
            pltpu.VMEM((2, 2048, 128), BF),
            pltpu.VMEM((2, 256, 2048), BF),
            pltpu.VMEM((2, 256, 2048), BF),
            pltpu.VMEM((chunks, 128, 512), BF),
            pltpu.VMEM((chunks, 128, 128), BF),
            pltpu.VMEM((256, 512), BF),
            pltpu.VMEM((2, 128, 2048), F32),
            pltpu.VMEM((256, 2048), BF),
            pltpu.VMEM((256, 2048), BF),
            pltpu.VMEM((2, zs - 1, 128, 512), BF),
            pltpu.VMEM((2, zs, 128, 512), BF),
            pltpu.VMEM((2, 128, 512), F32),
            pltpu.VMEM((2, 128, 512), BF),
            pltpu.VMEM((4, 64, 512), BF),
            pltpu.VMEM((2, 128, 2048), BF),
            pltpu.VMEM((2, 128, 512), BF),
            pltpu.VMEM((32, 128), F32),
            pltpu.VMEM((2, 16, 128), F32),
            pltpu.VMEM((blocks, 128), F32),
            pltpu.VMEM((2, blocks, 128), F32),
            dma((6,)), dma((6,)), dma((6,)), dma((2, 2)), dma((2, 2)), dma((3, 2)), dma((3, 2)),
            dma((2, zs - 1)), dma((2, zs - 1)), dma((2, zs - 1)), dma((2, zs - 1)),
            dma((3,)), dma((3,)), dma((3,)), dma((3,)), dma((3,)),
        ],
        compiler_params=pltpu.CompilerParams(
            collective_id=0, has_side_effects=True, vmem_limit_bytes=50 * 1024 * 1024
        ),
    )(q[0], o[0], g[0], ln[0], ok[0], ov[0], pk[0], pv[0], tab[0], lens)
    return tuple(out[None] for out in outs)


def solution(mesh):
    rows = P("pipe", "ctx", None)
    in_specs = (rows,) * 9 + (P("pipe", "ctx"),)
    fn = functools.partial(local, mesh.shape["ctx"] // 4, mesh.shape["pipe"])
    return jax.shard_map(fn, mesh=mesh, in_specs=in_specs, out_specs=(rows,) * 5, check_vma=False)
```

time: 446 us -> 124 us (0.28); the launches traced: 441 us -> 124 us
  waiting for transfers between devices: 246 us -> 0 us
  matrix products: 114 us -> 0 us
  Pallas kernels: 0 us -> 114 us
  local copies, waits for them, and re-layouts: 49.7 us -> 8.97 us
  between operations: 13.9 us -> 0.68 us
  starting transfers between devices: 6.08 us -> 0 us
  loops' own time: 6.03 us -> 0 us
  other arithmetic: 5.12 us -> 0 us
    all_gather x2 -> x0, waiting for transfers between devices: 115 us -> none  [the longest x1 63.6 us: local(): piece_values = lax.all_gather(pool_values, 'ctx', axis=1, tiled=True)]
    pallas_call x0 -> x1, Pallas kernels: none -> 114 us  [local(): pl.pallas_call(functools.partial(kernel, zs, pipes), out_shape=(jax.Shape...]
    dot_general x45 -> x0, matrix products: 114 us -> none  [the longest x9 33.2 us: key_terms(): jnp.einsum('hgrd,hnd->hgrn', grad_heads, value_heads, preferred_element_t...]
    reduce_scatter x1 -> x0, waiting for transfers between devices: 110 us -> none  [local(): lax.psum_scatter(partial_kv, 'ctx', scatter_dimension=0, tiled=True)]
    ppermute x1 -> x0, waiting for transfers between devices: 20.2 us -> none  [shifted(): return lax.ppermute(value, axis, pairs)]
    dynamic_slice x32 -> x0, local copies, waits for them, and re-layouts: 15.3 us -> none  [the longest x16 9.62 us: one_block(): block_values = lax.dynamic_slice_in_dim(value_rows, offset, block_size, 0)]
    dynamic_update_slice x16 -> x0, local copies, waits for them, and re-layouts: 11.2 us -> none  [key_sweep(): lax.scan(one_block, start_sum, jnp.arange(block_total, dtype=jnp.int32))]
    reshape x18 -> x0, local copies, waits for them, and re-layouts: 8.24 us -> none  [the longest x9 6.77 us: key_terms(): value_heads = value_rows.reshape(key_count, KVH, HD).transpose(1, 0, 2)]
  transfers between devices with their start and end apart: 4 -> 0, of which waited for: 4 -> 0; matrix products, arithmetic and copies ran while one was open for 4% -> 0% of each run, Pallas kernels for 0% -> 0%
where the time goes in v1:
time: 124 us
  Pallas kernels  114 us (92%)
  local copies, waits for them, and re-layouts  8.97 us (7%)
    pallas_call x1, Pallas kernels, local(): pl.pallas_call(functools.partial(kernel, zs, pipes), out_shape=(jax.Shape...  114 us
    unnamed x20, local copies, waits for them, and re-layouts  8.97 us

profile of v1, /device:TPU:1, one launch (start us, length us, event | category | flops | bytes accessed | tf_op | source)
XLA Modules:
  0.0 124.0 jit_solution(5029663048001962077)
XLA Ops:
  0.6 0.0 copy-start.3
  0.6 0.8 copy.15
  1.5 0.0 copy-start.5
  1.5 0.0 copy-start.6
  1.5 0.0 copy-done.3
  1.5 0.7 copy-done.5
  2.2 0.0 copy-done.6
  2.2 0.0 copy-start
  2.2 1.2 copy-done
  3.4 0.0 copy-start.1
  3.4 0.9 copy-done.1
  4.3 0.0 copy-start.2
  4.3 0.9 copy-done.2
  5.2 0.0 copy-start.4
  5.2 0.8 copy-done.4
  6.0 114.4 %shard_map.137 = (bf16[128,4096]{1,0:T(8,128)(2,1)S(1)}, bf16[128,512]{1,0:T(8,128)(2,1)S(1)}, bf16[128,512]{1,0:T(8,128)(2,1)S(1)}, f32[64,512]{1,0:T(8,128)S(1)}, f32[64,512]{1,0:T(8,128)S(1)}) custom-call(bf16[128,4096]{1,0:T(8,128)(2,1)S(1)} %bitcast.14, bf16[128,4096]{1,0:T(8,128)(2,1)} %bitcast.26, bf16[128,4096]{1,0:T(8,128)(2,1)} %bitcast.27, ...), custom_call_target="tpu_custom_call" | custom-call | tf_op jit(solution)/shard_map/pallas_call | solution.py:365
  120.4 1.0 copy.21
  121.4 0.7 copy.22
  122.0 0.7 copy.23
  122.7 0.7 copy.24
  123.4 0.7 copy.25
Async XLA Ops:
  0.6 0.9 copy-start.3
  1.5 0.7 copy-start.5
  1.5 0.7 copy-start.6
  2.2 1.2 copy-start
  3.4 0.9 copy-start.1
  4.3 0.9 copy-start.2
  5.2 0.8 copy-start.4

commit v2 on v1

v2 whole, which is shorter than its diff:
```python
import functools
import math

import jax
import jax.numpy as jnp
from jax import lax
from jax.experimental import pallas as pl
from jax.experimental.pallas import tpu as pltpu
from jax.sharding import PartitionSpec as P

HD = 128
ROWS = 128
RLEN = 64
BLK = 32
GROUP = 8
SCALE = HD ** -0.5
EXP_SCALE = SCALE * math.log2(math.e)
FAR = 1e30
BF = jnp.bfloat16
F32 = jnp.float32
MESH = pl.DeviceIdType.MESH


def split3(x):
    hi = x.astype(BF).astype(F32)
    rest = x - hi
    mid = rest.astype(BF).astype(F32)
    return hi, mid, rest - mid


def dot(a, b):
    return jnp.dot(a, b, preferred_element_type=F32)


def kernel(
    zs, pipes,
    q_hbm, o_hbm, g_hbm, ln_ref, ok_hbm, ov_hbm, pk_hbm, pv_hbm, tab_ref, len_ref,
    dq_out, dok_out, dov_out, dpk_out, dpv_out,
    qb, ob, cb, qh, ch, qt, ct, kv, kaug, okv, dqt, ds_s, p_s, part,
    send_buf, recv_buf, fsend, frecv, dq_st, ok_st, ln_t, ln_r, bp_s, bp,
    loc_sem, sib_send, sib_recv, cot_send, cot_recv, kv_send, kv_recv,
    ga_send, ga_recv, rs_send, rs_recv, f_send, f_recv, out_sem, out_send, out_recv,
):
    p = lax.axis_index("pipe")
    c = lax.axis_index("ctx")
    core = lax.rem(c, 2)
    z = lax.rem(lax.div(c, 2), zs)
    yl = lax.div(c, 2 * zs)
    oc = 1 - core
    hops = zs // 2

    def dev(pp, yy, zz, kk):
        return (pp, (yy * zs + zz) * 2 + kk)

    sib = dev(p, yl, z, oc)
    z_up = lax.rem(z + 1, zs)
    z_dn = lax.rem(z + zs - 1, zs)
    p_up = lax.rem(p + 1, pipes)
    p_dn = lax.rem(p + pipes - 1, pipes)
    ring_dst = (dev(p, yl, z_up, core), dev(p, yl, z_dn, core))

    def lanes_at(ref, start, width):
        return ref.at[:, pl.ds(pl.multiple_of(start, 128), width)]

    def remote(src, dst, ss, rs, to):
        return pltpu.make_async_remote_copy(
            src_ref=src, dst_ref=dst, send_sem=ss, recv_sem=rs, device_id=to, device_id_type=MESH
        )

    my_rows = pl.ds(pl.multiple_of(core * ROWS, ROWS), ROWS)
    my_keys = pl.ds(pl.multiple_of(yl * 128 + core * 64, 64), 64)

    loc = [
        pltpu.make_async_copy(lanes_at(q_hbm, core * 2048, 2048), qb.at[my_rows], loc_sem.at[0]),
        pltpu.make_async_copy(lanes_at(o_hbm, core * 2048, 2048), ob.at[my_rows], loc_sem.at[1]),
        pltpu.make_async_copy(lanes_at(ok_hbm, core * 256, 256), okv.at[my_rows, 0:256], loc_sem.at[2]),
        pltpu.make_async_copy(lanes_at(ov_hbm, core * 256, 256), okv.at[my_rows, 256:512], loc_sem.at[3]),
    ]
    kv_loc = [
        [
            pltpu.make_async_copy(
                lanes_at(src, core * 256 + h * 128, 128),
                kv.at[h, z, my_keys, j * 128 : (j + 1) * 128],
                loc_sem.at[4 + 2 * h + j],
            )
            for j, src in enumerate((pk_hbm, pv_hbm))
        ]
        for h in range(2)
    ]
    for cp in kv_loc[0] + kv_loc[1] + loc:
        cp.start()

    row = lax.broadcasted_iota(jnp.int32, (32, ROWS), 1)
    length = jnp.where(row < RLEN, len_ref[0, 0], len_ref[0, 1])
    live = lax.rem(row, RLEN) < length
    ln_t[...] = jnp.where(live, ln_ref[...] * (1.0 / SCALE), FAR)
    lane = lax.broadcasted_iota(jnp.int32, bp_s.shape, 1)
    ids = lax.broadcasted_iota(jnp.int32, (bp_s.shape[0], tab_ref.shape[1]), 0)
    offs = jnp.zeros(bp_s.shape, F32)
    for rr in range(2):
        hit = jnp.where(tab_ref[rr : rr + 1, :] == ids, 1.0, 0.0)
        listed = jnp.max(hit, axis=1, keepdims=True)
        offs = jnp.where(lane == 3 + 2 * core + rr, (listed - 1.0) * FAR, offs)
    bp_s[...] = offs
    bp[core] = offs
    ln_r[core] = ln_t[pl.ds(pl.multiple_of(core * 16, 16), 16), :]

    barrier = pltpu.get_barrier_semaphore()
    partners = [
        sib,
        dev(p, 1 - yl, z, 0), dev(p, 1 - yl, z, 1),
        ring_dst[0], ring_dst[1],
        dev(p_dn, yl, z, 0), dev(p_dn, yl, z, 1),
        dev(p_up, yl, z, 0), dev(p_up, yl, z, 1),
    ]
    for to in partners:
        pl.semaphore_signal(barrier, inc=1, device_id=to, device_id_type=MESH)
    pl.semaphore_wait(barrier, len(partners))

    group = [(yl, oc), (1 - yl, core), (1 - yl, oc)]
    kv_out = [
        [
            remote(
                lanes_at(src, kk * 256 + h * 128, 128),
                kv.at[h, z, my_keys, j * 128 : (j + 1) * 128],
                kv_send.at[i, h, j], kv_recv.at[i, h, j], dev(p, yy, z, kk),
            )
            for i, (yy, kk) in enumerate(group)
            for j, src in enumerate((pk_hbm, pv_hbm))
        ]
        for h in range(2)
    ]
    for cp in kv_out[0] + kv_out[1]:
        cp.start()

    sib_out = [
        remote(lanes_at(q_hbm, oc * 2048, 2048), qb.at[my_rows], sib_send.at[0], sib_recv.at[0], sib),
        remote(lanes_at(o_hbm, oc * 2048, 2048), ob.at[my_rows], sib_send.at[1], sib_recv.at[1], sib),
        remote(lanes_at(ok_hbm, oc * 256, 256), okv.at[my_rows, 0:256], sib_send.at[2], sib_recv.at[2], sib),
        remote(lanes_at(ov_hbm, oc * 256, 256), okv.at[my_rows, 256:512], sib_send.at[3], sib_recv.at[3], sib),
        remote(ln_t.at[pl.ds(pl.multiple_of(oc * 16, 16), 16)], ln_r.at[core], sib_send.at[4], sib_recv.at[4], sib),
        remote(bp_s, bp.at[core], sib_send.at[5], sib_recv.at[5], sib),
    ]
    for i in (4, 5, 0, 2, 3, 1):
        sib_out[i].start()

    cot_out = [
        [
            remote(
                lanes_at(g_hbm, kk * 2048 + h * 1024, 1024),
                cb.at[my_rows, h * 1024 : (h + 1) * 1024],
                cot_send.at[h, d], cot_recv.at[h, d], dev(p_dn, yl, z, kk),
            )
            for d, kk in enumerate((oc, core))
        ]
        for h in range(2)
    ]

    def gather(h, d, t):
        chunk = lax.rem(z + zs - (t - 1), zs) if d == 0 else lax.rem(z + t - 1, zs)
        rows = slice(0, 256) if t < hops else slice(d * 128, (d + 1) * 128)
        ref = kv.at[h, chunk, rows]
        return remote(ref, ref, ga_send.at[h, d, t - 1], ga_recv.at[h, d, t - 1], ring_dst[d])

    def gather_wait(h, d, t):
        chunk = lax.rem(z + zs - t, zs) if d == 0 else lax.rem(z + t, zs)
        rows = slice(0, 256) if t < hops else slice(d * 128, (d + 1) * 128)
        ref = kv.at[h, chunk, rows]
        remote(ref, ref, ga_send.at[h, d, t - 1], ga_recv.at[h, d, t - 1], ring_dst[d]).wait_recv()

    def gather_pass(h, t):
        for d in range(2):
            gather_wait(h, d, t)
            if t < hops:
                gather(h, d, t + 1).start()

    for h in range(2):
        for cp in kv_loc[h]:
            cp.wait()
        for cp in kv_out[h]:
            cp.wait_recv()
        for d in range(2):
            gather(h, d, 1).start()
    for cp in cot_out[0]:
        cp.start()

    qt[:, 128:256, :] = jnp.zeros((2, 128, 2048), BF)
    ct[:, 128:256, :] = jnp.zeros((2, 128, 2048), BF)
    dqt[...] = jnp.zeros(dqt.shape, F32)
    sub = lax.broadcasted_iota(jnp.int32, (16, 128), 0)
    col = lax.broadcasted_iota(jnp.int32, (16, 128), 1)

    def tile_cols(side, g):
        return slice(side * 1024 + g * 128, side * 1024 + (g + 1) * 128)

    def query_tiles(h, side):
        for g in range(GROUP):
            cols = tile_cols(side, g)
            tile = qb[side * 128 : (side + 1) * 128, (h * 8 + g) * 128 : (h * 8 + g + 1) * 128]
            qh[h, cols, :] = tile
            qt[h, 0:128, cols] = tile.T
            hi, mid, low = split3(ln_r[side, h * 8 + g : h * 8 + g + 1, :])
            own = jnp.where(sub - 3 == side * 2 + lax.div(col, RLEN), 1.0, 0.0)
            aug = jnp.where(sub == 0, -hi, jnp.where(sub == 1, -mid, jnp.where(sub == 2, -low, own)))
            qt[h, 128:144, cols] = aug.astype(BF)

    def cot_tiles(h, side):
        for g in range(GROUP):
            cols = tile_cols(side, g)
            rows, lanes = slice(side * 128, (side + 1) * 128), slice((h * 8 + g) * 128, (h * 8 + g + 1) * 128)
            tile = cb[rows, lanes]
            ch[h, cols, :] = tile
            tile_t = tile.T
            ct[h, 0:128, cols] = tile_t
            prod = tile_t.astype(F32) * ob[rows, lanes].T.astype(F32)
            hi, mid, low = split3(jnp.sum(prod, axis=0, keepdims=True))
            aug = jnp.where(sub == 0, hi, jnp.where(sub == 1, mid, jnp.where(sub == 2, low, 0.0)))
            ct[h, 128:144, cols] = aug.astype(BF)

    sib_out[4].wait_recv()
    sib_out[5].wait_recv()
    aug_lane = lax.broadcasted_iota(jnp.int32, bp_s.shape, 1)
    blocks = bp[0] + bp[1] + jnp.where(aug_lane < 3, 1.0, 0.0)
    spread = jnp.broadcast_to(blocks[:, None, :], (blocks.shape[0], BLK, 128))
    spread = spread.reshape(2, zs, 128, 128).astype(BF)
    for yy in range(2):
        kaug[:, yy * 128 : (yy + 1) * 128, :] = spread[yy]

    def second_cot():
        for cp in cot_out[0]:
            cp.wait_send()
        for cp in cot_out[1]:
            cp.start()

    loc[0].wait()
    sib_out[0].wait_recv()
    for side in range(2):
        query_tiles(0, side)
    for t in range(1, hops - 1):
        gather_pass(0, t)
        if t == 1:
            for side in range(2):
                query_tiles(1, side)
        if t == hops - 2:
            second_cot()
        gather_pass(1, t)
    if hops < 3:
        for side in range(2):
            query_tiles(1, side)
        second_cot()

    loc[1].wait()
    for i in (1, 2, 3):
        sib_out[i].wait_recv()
    loc[2].wait()
    loc[3].wait()

    one_lane = lax.broadcasted_iota(jnp.int32, (256, 128), 1) < 3
    v_cst = jnp.where(one_lane, -1.0, 0.0).astype(BF)
    k_cst = jnp.where(one_lane, 1.0, 0.0).astype(BF)

    def own_part(h):
        key_i = lax.broadcasted_iota(jnp.int32, (ROWS, 1024), 0)
        row_i = lax.rem(lax.broadcasted_iota(jnp.int32, (ROWS, 1024), 1), ROWS)
        seen = (lax.div(key_i, RLEN) == lax.div(row_i, RLEN)) & (key_i <= row_i)
        for side in range(2):
            rows = slice(side * 128, (side + 1) * 128)
            cols = slice(side * 1024, (side + 1) * 1024)
            k_l = okv[rows, h * 128 : (h + 1) * 128]
            v_l = okv[rows, 256 + h * 128 : 256 + (h + 1) * 128]
            s = dot(jnp.concatenate([k_l, k_cst[:128]], 1), qt[h, :, cols])
            pr = jnp.where(seen, jnp.exp2(s * EXP_SCALE), 0.0)
            dp = dot(jnp.concatenate([v_l, v_cst[:128]], 1), ct[h, :, cols])
            ds = (pr * dp).astype(BF)
            dqt[h, :, cols] += dot(k_l.T, ds)
            ok_st[side, :, h * 128 : (h + 1) * 128] = (dot(ds, qh[h, cols, :]) * SCALE).astype(BF)
            ok_st[side, :, 256 + h * 128 : 256 + (h + 1) * 128] = dot(pr.astype(BF), ch[h, cols, :]).astype(BF)

    def unit(h, j):
        offset = lax.div(j + 1, 2) * (1 - 2 * lax.rem(j, 2))
        chunk = lax.rem(z + zs + offset, zs)
        k_l = kv[h, chunk, :, 0:128]
        k_full = jnp.concatenate([k_l, kaug[chunk]], 1)
        v_full = jnp.concatenate([kv[h, chunk, :, 128:256], v_cst], 1)
        for n in range(4):
            cols = slice(n * 512, (n + 1) * 512)
            pr = jnp.exp2(dot(k_full, qt[h, :, cols]) * EXP_SCALE)
            dp = dot(v_full, ct[h, :, cols])
            p_s[:, cols] = pr.astype(BF)
            ds_s[:, cols] = (pr * dp).astype(BF)
        dqt[h] += dot(k_l.T, ds_s[...])
        part[h, j, :, 0:128] = dot(ds_s[...], qh[h])
        part[h, j, :, 128:256] = dot(p_s[...], ch[h])

    def rs_rows(d, k):
        return slice(0, 256) if k < hops else slice(d * 128, (d + 1) * 128)

    def rs_copy(h, d, k):
        rows = rs_rows(d, k)
        return remote(
            send_buf.at[h, d, k - 1, rows], recv_buf.at[h, d, k - 1, rows],
            rs_send.at[h, d, k - 1], rs_recv.at[h, d, k - 1], ring_dst[d],
        )

    def rs_stage(h, d, k):
        j = zs - 1 if k == hops else (2 * k if d == 0 else 2 * k - 1)
        rows = rs_rows(d, k)
        send_buf[h, d, k - 1, rows] = part[h, j, rows].astype(BF)
        if k < hops:
            rs_copy(h, d, k + 1).wait_recv()
            got = rs_rows(d, k + 1)
            total = part[h, j, got] + recv_buf[h, d, k, got].astype(F32)
            send_buf[h, d, k - 1, got] = total.astype(BF)
        rs_copy(h, d, k).start()

    me4 = yl * 2 + core
    f_out = [
        [
            remote(
                fsend.at[h, pl.ds(pl.multiple_of(yy * 128 + kk * 64, 64), 64)],
                frecv.at[h, me4], f_send.at[h, i], f_recv.at[h, i], dev(p, yy, z, kk),
            )
            for i, (yy, kk) in enumerate(group)
        ]
        for h in range(2)
    ]

    def rs_last(h):
        total = part[h, 0]
        for d in range(2):
            rs_copy(h, d, 1).wait_recv()
            got = rs_rows(d, 1)
            if hops == 1:
                part[h, 0, got] += recv_buf[h, d, 0, got].astype(F32)
                total = part[h, 0]
            else:
                total = total + recv_buf[h, d, 0].astype(F32)
        fsend[h] = total.astype(BF)
        for cp in f_out[h]:
            cp.start()
        frecv[h, me4] = fsend[h, my_keys, :]

    def f_finish(h):
        for cp in f_out[h]:
            cp.wait_recv()
        for kk in range(2):
            tot = frecv[h, kk].astype(F32) + frecv[h, 2 + kk].astype(F32)
            lanes = slice((2 * kk + h) * 128, (2 * kk + h + 1) * 128)
            dpk_out[:, lanes] = tot[:, 0:128] * SCALE
            dpv_out[:, lanes] = tot[:, 128:256]

    def dq_tiles(h):
        for side in range(2):
            for g in range(GROUP):
                tile = dqt[h, :, tile_cols(side, g)] * SCALE
                dq_st[side, :, (h * 8 + g) * 128 : (h * 8 + g + 1) * 128] = tile.T.astype(BF)

    def dq_copies(h):
        lanes = slice(h * 1024, (h + 1) * 1024)
        dst = lanes_at(dq_out, core * 2048 + h * 1024, 1024)
        return [
            remote(dq_st.at[oc, :, lanes], dst, out_send.at[2 + h], out_recv.at[2 + h], sib),
            pltpu.make_async_copy(dq_st.at[core, :, lanes], dst, out_sem.at[2 + h]),
        ]

    for cp in cot_out[0]:
        cp.wait_recv()
    for side in range(2):
        cot_tiles(0, side)
    own_part(0)
    first = zs - 3

    def pass0(i, carry):
        late = jnp.minimum(lax.div(i, first), 1)
        j = (1 - late) * i + late * (first + lax.rem(i - first + 2 + 3 * zs, 3))

        @pl.when(i == first - 1)
        def _():
            for h in range(2):
                gather_pass(h, hops - 1)

        @pl.when(i == first)
        def _():
            gather_pass(0, hops)

        unit(0, j)

        @pl.when(i == first)
        def _():
            for d in range(2):
                rs_stage(0, d, hops)

        for d in range(2):
            @pl.when(i == zs - 1 - d)
            def _(d=d):
                rs_stage(0, d, hops - 1)

        return carry

    lax.fori_loop(0, zs, pass0, 0)

    gather_pass(1, hops)
    for cp in cot_out[1]:
        cp.wait_recv()
    for side in range(2):
        cot_tiles(1, side)

    def pass1(i, carry):
        unit(1, zs - 1 - i)

        @pl.when(i == 0)
        def _():
            for d in range(2):
                rs_stage(1, d, hops)

        for k in range(hops - 1, 0, -1):
            for d in range(2):
                @pl.when(i == 2 * (hops - k) - 1 + d)
                def _(d=d, k=k):
                    rs_stage(1, d, k)

            if k < hops - 1:
                @pl.when(i == 2 * (hops - 1 - k))
                def _(k=k):
                    for d in range(2):
                        rs_stage(0, d, k)

        return carry

    lax.fori_loop(0, zs, pass1, 0)

    rs_last(0)
    own_part(1)
    ok_out = []
    for j, out in enumerate((dok_out, dov_out)):
        lanes = slice(j * 256, (j + 1) * 256)
        dst = lanes_at(out, core * 256, 256)
        ok_out.append(remote(ok_st.at[oc, :, lanes], dst, out_send.at[j], out_recv.at[j], sib))
        ok_out.append(pltpu.make_async_copy(ok_st.at[core, :, lanes], dst, out_sem.at[j]))
    for cp in ok_out:
        cp.start()
    for h in range(2):
        dq_tiles(h)
        for cp in dq_copies(h):
            cp.start()
    rs_last(1)
    f_finish(0)
    for cp in ok_out + dq_copies(0) + dq_copies(1):
        cp.wait()
    for cp in kv_out[0] + kv_out[1] + cot_out[1] + sib_out + f_out[0]:
        cp.wait_send()
    for h in range(2):
        for d in range(2):
            for t in range(1, hops + 1):
                gather(h, d, t).wait_send()
                rs_copy(h, d, t).wait_send()
    f_finish(1)
    for cp in f_out[1]:
        cp.wait_send()


def hand_over(*refs):
    for src, dst in zip(refs[:5], refs[5:]):
        dst[...] = src[...]


def local(zs, pipes, q, o, g, ln, ok, ov, pk, pv, tab, lens):
    any_ = pl.BlockSpec(memory_space=pl.ANY)
    vmem = pl.BlockSpec(memory_space=pltpu.VMEM)
    smem = pl.BlockSpec(memory_space=pltpu.SMEM)
    hops = zs // 2
    blocks = zs * 256 // BLK
    dma = pltpu.SemaphoreType.DMA
    outs = pl.pallas_call(
        functools.partial(kernel, zs, pipes),
        out_shape=(
            jax.ShapeDtypeStruct((ROWS, 4096), BF),
            jax.ShapeDtypeStruct((ROWS, 512), BF),
            jax.ShapeDtypeStruct((ROWS, 512), BF),
            jax.ShapeDtypeStruct((64, 512), F32),
            jax.ShapeDtypeStruct((64, 512), F32),
        ),
        in_specs=[any_, any_, any_, vmem, any_, any_, any_, any_, vmem, smem],
        out_specs=(any_, any_, any_, vmem, vmem),
        scratch_shapes=[
            pltpu.VMEM((256, 2048), BF),
            pltpu.VMEM((256, 2048), BF),
            pltpu.VMEM((256, 2048), BF),
            pltpu.VMEM((2, 2048, 128), BF),
            pltpu.VMEM((2, 2048, 128), BF),
            pltpu.VMEM((2, 256, 2048), BF),
            pltpu.VMEM((2, 256, 2048), BF),
            pltpu.VMEM((2, zs, 256, 256), BF),
            pltpu.VMEM((zs, 256, 128), BF),
            pltpu.VMEM((256, 512), BF),
            pltpu.VMEM((2, 128, 2048), F32),
            pltpu.VMEM((256, 2048), BF),
            pltpu.VMEM((256, 2048), BF),
            pltpu.VMEM((2, zs, 256, 256), F32),
            pltpu.VMEM((2, 2, hops, 256, 256), BF),
            pltpu.VMEM((2, 2, hops, 256, 256), BF),
            pltpu.VMEM((2, 256, 256), BF),
            pltpu.VMEM((2, 4, 64, 256), BF),
            pltpu.VMEM((2, 128, 2048), BF),
            pltpu.VMEM((2, 128, 512), BF),
            pltpu.VMEM((32, 128), F32),
            pltpu.VMEM((2, 16, 128), F32),
            pltpu.VMEM((blocks, 128), F32),
            pltpu.VMEM((2, blocks, 128), F32),
            dma((8,)), dma((6,)), dma((6,)), dma((2, 2)), dma((2, 2)), dma((3, 2, 2)), dma((3, 2, 2)),
            dma((2, 2, hops)), dma((2, 2, hops)), dma((2, 2, hops)), dma((2, 2, hops)),
            dma((2, 3)), dma((2, 3)), dma((4,)), dma((4,)), dma((4,)),
        ],
        compiler_params=pltpu.CompilerParams(
            collective_id=0, has_side_effects=True, vmem_limit_bytes=56 * 1024 * 1024
        ),
    )(q[0], o[0], g[0], ln[0].T, ok[0], ov[0], pk[0], pv[0], tab[0], lens)
    outs = pl.pallas_call(
        hand_over,
        out_shape=tuple(jax.ShapeDtypeStruct(out.shape, out.dtype) for out in outs),
        in_specs=[vmem] * 5,
        out_specs=(vmem,) * 5,
    )(*outs)
    return tuple(out[None] for out in outs)


def solution(mesh):
    rows = P("pipe", "ctx", None)
    in_specs = (rows,) * 9 + (P("pipe", "ctx"),)
    fn = functools.partial(local, mesh.shape["ctx"] // 4, mesh.shape["pipe"])
    return jax.shard_map(fn, mesh=mesh, in_specs=in_specs, out_specs=(rows,) * 5, check_vma=False)
```

time: 124 us -> 79.2 us (0.64)
  Pallas kernels: 114 us -> 77.5 us
  local copies, waits for them, and re-layouts: 8.97 us -> 0 us
    pallas_call x1, Pallas kernels: 114 us -> 75 us  [local(): pl.pallas_call(functools.partial(kernel, zs, pipes), out_shape=(jax.Shape...]
    unnamed x20 -> x0, local copies, waits for them, and re-layouts: 8.97 us -> none
    pallas_call x0 -> x1, Pallas kernels: none -> 2.53 us  [local(): pl.pallas_call(hand_over, out_shape=tuple((jax.ShapeDtypeStruct(out.shape...]
where the time goes in v2:
time: 79.2 us; the launch traced here: 78.2 us
  Pallas kernels  77.5 us (98%)
    pallas_call x1, Pallas kernels, local(): pl.pallas_call(functools.partial(kernel, zs, pipes), out_shape=(jax.Shape...  75 us
    pallas_call x1, Pallas kernels, local(): pl.pallas_call(hand_over, out_shape=tuple((jax.ShapeDtypeStruct(out.shape...  2.53 us

profile of v2, /device:TPU:1, one launch (start us, length us, event | category | flops | bytes accessed | tf_op | source)
XLA Modules:
  0.0 78.2 jit_solution(14708096456218083081)
XLA Ops:
  0.6 75.0 %shard_map.137 = (bf16[128,4096]{1,0:T(8,128)(2,1)}, bf16[128,512]{1,0:T(8,128)(2,1)}, bf16[128,512]{1,0:T(8,128)(2,1)}, f32[64,512]{1,0:T(8,128)}, f32[64,512]{1,0:T(8,128)}) custom-call(bf16[128,4096]{1,0:T(8,128)(2,1)} %bitcast.16, bf16[128,4096]{1,0:T(8,128)(2,1)} %bitcast.17, bf16[128,4096]{1,0:T(8,128)(2,1)} %bitcast.18, f32[32,128]{1,0:T(8,128)} %bitcast.23, ...), custom_call_target="tpu_custom_call" | custom-call | tf_op jit(solution)/shard_map/pallas_call | solution.py:474
  75.6 2.5 %shard_map.138 = (bf16[128,4096]{1,0:T(8,128)(2,1)}, bf16[128,512]{1,0:T(8,128)(2,1)}, bf16[128,512]{1,0:T(8,128)(2,1)}, f32[64,512]{1,0:T(8,128)}, f32[64,512]{1,0:T(8,128)}) custom-call(bf16[128,4096]{1,0:T(8,128)(2,1)} %get-tuple-element.15.refs_0_, bf16[128,512]{1,0:T(8,128)(2,1)} %get-tuple-element.16.refs_1_, ...), custom_call_target="tpu_custom_call" | custom-call | tf_op jit(solution)/shard_map/pallas_call | solution.py:518

commit v3 on v2

--- a/solution.py
+++ b/solution.py
@@ -37,9 +37,9 @@
     q_hbm, o_hbm, g_hbm, ln_ref, ok_hbm, ov_hbm, pk_hbm, pv_hbm, tab_ref, len_ref,
     dq_out, dok_out, dov_out, dpk_out, dpv_out,
     qb, ob, cb, qh, ch, qt, ct, kv, kaug, okv, dqt, ds_s, p_s, part,
-    send_buf, recv_buf, fsend, frecv, dq_st, ok_st, ln_t, ln_r, bp_s, bp,
+    send_buf, recv_buf, y_buf, y_got, z_buf, z_got, fsend, frecv, fsum, fgot, dq_st, ok_st, ln_t, ln_r, bp_s, bp,
     loc_sem, sib_send, sib_recv, cot_send, cot_recv, kv_send, kv_recv,
-    ga_send, ga_recv, rs_send, rs_recv, f_send, f_recv, out_sem, out_send, out_recv,
+    ga_send, ga_recv, rs_send, rs_recv, y_send, y_recv, z_send, z_recv, f_send, f_recv, out_sem, out_send, out_recv,
 ):
     p = lax.axis_index("pipe")
     c = lax.axis_index("ctx")
@@ -147,14 +147,24 @@
     cot_out = [
         [
             remote(
-                lanes_at(g_hbm, kk * 2048 + h * 1024, 1024),
-                cb.at[my_rows, h * 1024 : (h + 1) * 1024],
-                cot_send.at[h, d], cot_recv.at[h, d], dev(p_dn, yl, z, kk),
+                lanes_at(g_hbm, kk * 2048 + part_i * 512, 512),
+                cb.at[my_rows, part_i * 512 : (part_i + 1) * 512],
+                cot_send.at[part_i, d], cot_recv.at[part_i, d], dev(p_dn, yl, z, kk),
             )
             for d, kk in enumerate((oc, core))
         ]
-        for h in range(2)
+        for part_i in range(4)
     ]
+
+    def cot_next(done):
+        for cp in cot_out[done]:
+            cp.wait_send()
+        for cp in cot_out[done + 1]:
+            cp.start()
+
+    def cot_wait(i):
+        for cp in cot_out[i]:
+            cp.wait_recv()
 
     def gather(h, d, t):
         chunk = lax.rem(z + zs - (t - 1), zs) if d == 0 else lax.rem(z + t - 1, zs)
@@ -191,7 +201,8 @@
     col = lax.broadcasted_iota(jnp.int32, (16, 128), 1)
 
     def tile_cols(side, g):
-        return slice(side * 1024 + g * 128, side * 1024 + (g + 1) * 128)
+        start = (g // 4) * 1024 + side * 512 + (g % 4) * 128
+        return slice(start, start + 128)
 
     def query_tiles(h, side):
         for g in range(GROUP):
@@ -204,8 +215,8 @@
             aug = jnp.where(sub == 0, -hi, jnp.where(sub == 1, -mid, jnp.where(sub == 2, -low, own)))
             qt[h, 128:144, cols] = aug.astype(BF)
 
-    def cot_tiles(h, side):
-        for g in range(GROUP):
+    def cot_tiles(h, q):
+        for side, g in [(side, g) for side in range(2) for g in range(q * 4, q * 4 + 4)]:
             cols = tile_cols(side, g)
             rows, lanes = slice(side * 128, (side + 1) * 128), slice((h * 8 + g) * 128, (h * 8 + g + 1) * 128)
             tile = cb[rows, lanes]
@@ -226,28 +237,17 @@
     for yy in range(2):
         kaug[:, yy * 128 : (yy + 1) * 128, :] = spread[yy]
 
-    def second_cot():
-        for cp in cot_out[0]:
-            cp.wait_send()
-        for cp in cot_out[1]:
-            cp.start()
-
     loc[0].wait()
     sib_out[0].wait_recv()
     for side in range(2):
         query_tiles(0, side)
-    for t in range(1, hops - 1):
-        gather_pass(0, t)
-        if t == 1:
-            for side in range(2):
-                query_tiles(1, side)
-        if t == hops - 2:
-            second_cot()
-        gather_pass(1, t)
-    if hops < 3:
-        for side in range(2):
-            query_tiles(1, side)
-        second_cot()
+    if hops > 2:
+        gather_pass(0, 1)
+    for side in range(2):
+        query_tiles(1, side)
+    cot_next(0)
+    if hops > 2:
+        gather_pass(1, 1)
 
     loc[1].wait()
     for i in (1, 2, 3):
@@ -260,94 +260,161 @@
     k_cst = jnp.where(one_lane, 1.0, 0.0).astype(BF)
 
     def own_part(h):
-        key_i = lax.broadcasted_iota(jnp.int32, (ROWS, 1024), 0)
-        row_i = lax.rem(lax.broadcasted_iota(jnp.int32, (ROWS, 1024), 1), ROWS)
+        key_i = lax.broadcasted_iota(jnp.int32, (ROWS, 512), 0)
+        row_i = lax.rem(lax.broadcasted_iota(jnp.int32, (ROWS, 512), 1), ROWS)
         seen = (lax.div(key_i, RLEN) == lax.div(row_i, RLEN)) & (key_i <= row_i)
         for side in range(2):
             rows = slice(side * 128, (side + 1) * 128)
-            cols = slice(side * 1024, (side + 1) * 1024)
             k_l = okv[rows, h * 128 : (h + 1) * 128]
             v_l = okv[rows, 256 + h * 128 : 256 + (h + 1) * 128]
-            s = dot(jnp.concatenate([k_l, k_cst[:128]], 1), qt[h, :, cols])
-            pr = jnp.where(seen, jnp.exp2(s * EXP_SCALE), 0.0)
-            dp = dot(jnp.concatenate([v_l, v_cst[:128]], 1), ct[h, :, cols])
-            ds = (pr * dp).astype(BF)
-            dqt[h, :, cols] += dot(k_l.T, ds)
-            ok_st[side, :, h * 128 : (h + 1) * 128] = (dot(ds, qh[h, cols, :]) * SCALE).astype(BF)
-            ok_st[side, :, 256 + h * 128 : 256 + (h + 1) * 128] = dot(pr.astype(BF), ch[h, cols, :]).astype(BF)
-
-    def unit(h, j):
+            k_full = jnp.concatenate([k_l, k_cst[:128]], 1)
+            v_full = jnp.concatenate([v_l, v_cst[:128]], 1)
+            dk = jnp.zeros((ROWS, HD), F32)
+            dv = jnp.zeros((ROWS, HD), F32)
+            for q in range(2):
+                cols = slice(q * 1024 + side * 512, q * 1024 + (side + 1) * 512)
+                pr = jnp.where(seen, jnp.exp2(dot(k_full, qt[h, :, cols]) * EXP_SCALE), 0.0)
+                ds = (pr * dot(v_full, ct[h, :, cols])).astype(BF)
+                dqt[h, :, cols] += dot(k_l.T, ds)
+                dk += dot(ds, qh[h, cols, :])
+                dv += dot(pr.astype(BF), ch[h, cols, :])
+            ok_st[side, :, h * 128 : (h + 1) * 128] = (dk * SCALE).astype(BF)
+            ok_st[side, :, 256 + h * 128 : 256 + (h + 1) * 128] = dv.astype(BF)
+
+    def unit(h, j, q=None):
+        lo, hi = (0, 2048) if q is None else (q * 1024, (q + 1) * 1024)
         offset = lax.div(j + 1, 2) * (1 - 2 * lax.rem(j, 2))
         chunk = lax.rem(z + zs + offset, zs)
         k_l = kv[h, chunk, :, 0:128]
         k_full = jnp.concatenate([k_l, kaug[chunk]], 1)
         v_full = jnp.concatenate([kv[h, chunk, :, 128:256], v_cst], 1)
-        for n in range(4):
-            cols = slice(n * 512, (n + 1) * 512)
+        for n in range(lo, hi, 512):
+            cols = slice(n, n + 512)
             pr = jnp.exp2(dot(k_full, qt[h, :, cols]) * EXP_SCALE)
             dp = dot(v_full, ct[h, :, cols])
             p_s[:, cols] = pr.astype(BF)
             ds_s[:, cols] = (pr * dp).astype(BF)
-        dqt[h] += dot(k_l.T, ds_s[...])
-        part[h, j, :, 0:128] = dot(ds_s[...], qh[h])
-        part[h, j, :, 128:256] = dot(p_s[...], ch[h])
+        dqt[h, :, lo:hi] += dot(k_l.T, ds_s[:, lo:hi])
+        dk = dot(ds_s[:, lo:hi], qh[h, lo:hi])
+        dv = dot(p_s[:, lo:hi], ch[h, lo:hi])
+        if q == 1:
+            part[h, j, :, 0:128] += dk
+            part[h, j, :, 128:256] += dv
+        else:
+            part[h, j, :, 0:128] = dk
+            part[h, j, :, 128:256] = dv
 
     def rs_rows(d, k):
         return slice(0, 256) if k < hops else slice(d * 128, (d + 1) * 128)
 
-    def rs_copy(h, d, k):
+    def place(d, k):
+        return zs - 1 if k == hops else (2 * k if d == 0 else 2 * k - 1)
+
+    def rs_copy(d, k):
         rows = rs_rows(d, k)
         return remote(
-            send_buf.at[h, d, k - 1, rows], recv_buf.at[h, d, k - 1, rows],
-            rs_send.at[h, d, k - 1], rs_recv.at[h, d, k - 1], ring_dst[d],
+            send_buf.at[d, k - 1, rows], recv_buf.at[d, k - 1, rows],
+            rs_send.at[d, k - 1], rs_recv.at[d, k - 1], ring_dst[d],
         )
 
-    def rs_stage(h, d, k):
-        j = zs - 1 if k == hops else (2 * k if d == 0 else 2 * k - 1)
+    def rs_stage(d, k):
+        j = place(d, k)
         rows = rs_rows(d, k)
-        send_buf[h, d, k - 1, rows] = part[h, j, rows].astype(BF)
+        send_buf[d, k - 1, rows] = part[0, j, rows].astype(BF)
         if k < hops:
-            rs_copy(h, d, k + 1).wait_recv()
+            rs_copy(d, k + 1).wait_recv()
             got = rs_rows(d, k + 1)
-            total = part[h, j, got] + recv_buf[h, d, k, got].astype(F32)
-            send_buf[h, d, k - 1, got] = total.astype(BF)
-        rs_copy(h, d, k).start()
+            total = part[0, j, got] + recv_buf[d, k, got].astype(F32)
+            send_buf[d, k - 1, got] = total.astype(BF)
+        rs_copy(d, k).start()
 
     me4 = yl * 2 + core
     f_out = [
-        [
-            remote(
-                fsend.at[h, pl.ds(pl.multiple_of(yy * 128 + kk * 64, 64), 64)],
-                frecv.at[h, me4], f_send.at[h, i], f_recv.at[h, i], dev(p, yy, z, kk),
-            )
-            for i, (yy, kk) in enumerate(group)
-        ]
-        for h in range(2)
+        remote(
+            fsend.at[pl.ds(pl.multiple_of(yy * 128 + kk * 64, 64), 64)],
+            frecv.at[me4], f_send.at[i], f_recv.at[i], dev(p, yy, z, kk),
+        )
+        for i, (yy, kk) in enumerate(group)
     ]
 
-    def rs_last(h):
-        total = part[h, 0]
+    def rs_last():
         for d in range(2):
-            rs_copy(h, d, 1).wait_recv()
+            rs_copy(d, 1).wait_recv()
             got = rs_rows(d, 1)
-            if hops == 1:
-                part[h, 0, got] += recv_buf[h, d, 0, got].astype(F32)
-                total = part[h, 0]
-            else:
-                total = total + recv_buf[h, d, 0].astype(F32)
-        fsend[h] = total.astype(BF)
-        for cp in f_out[h]:
+            part[0, 0, got] += recv_buf[d, 0, got].astype(F32)
+        fsend[...] = part[0, 0].astype(BF)
+        for cp in f_out:
             cp.start()
-        frecv[h, me4] = fsend[h, my_keys, :]
-
-    def f_finish(h):
-        for cp in f_out[h]:
+        frecv[me4] = fsend[my_keys, :]
+
+    def pool_out(h, kk, tot):
+        lanes = slice((2 * kk + h) * 128, (2 * kk + h + 1) * 128)
+        dpk_out[:, lanes] = tot[:, 0:128] * SCALE
+        dpv_out[:, lanes] = tot[:, 128:256]
+
+    def rs_finish():
+        for cp in f_out:
             cp.wait_recv()
         for kk in range(2):
-            tot = frecv[h, kk].astype(F32) + frecv[h, 2 + kk].astype(F32)
-            lanes = slice((2 * kk + h) * 128, (2 * kk + h + 1) * 128)
-            dpk_out[:, lanes] = tot[:, 0:128] * SCALE
-            dpv_out[:, lanes] = tot[:, 128:256]
+            pool_out(0, kk, frecv[kk].astype(F32) + frecv[2 + kk].astype(F32))
+
+    def y_copy(j):
+        return remote(y_buf.at[j], y_got.at[j], y_send.at[j], y_recv.at[j], dev(p, 1 - yl, z, core))
+
+    def own_rows(rows):
+        return pl.ds(pl.multiple_of(yl * 128 + rows.start, 64), rows.stop - rows.start)
+
+    def y_start(j):
+        other = pl.ds(pl.multiple_of((1 - yl) * 128, 128), 128)
+        y_buf[j] = part[1, j, other].astype(BF)
+        y_copy(j).start()
+
+    def y_add(j):
+        y_copy(j).wait_recv()
+        mine = own_rows(slice(0, 128))
+        part[1, j, mine] = part[1, j, mine] + y_got[j].astype(F32)
+
+    def z_rows(d, k):
+        return slice(0, 128) if k < hops else slice(d * 64, (d + 1) * 64)
+
+    def z_copy(d, k):
+        rows = z_rows(d, k)
+        return remote(
+            z_buf.at[d, k - 1, rows], z_got.at[d, k - 1, rows],
+            z_send.at[d, k - 1], z_recv.at[d, k - 1], ring_dst[d],
+        )
+
+    def z_stage(d, k):
+        j = place(d, k)
+        rows = z_rows(d, k)
+        if k < hops or d == 0:
+            y_add(j)
+        z_buf[d, k - 1, rows] = part[1, j, own_rows(rows)].astype(BF)
+        if k < hops:
+            z_copy(d, k + 1).wait_recv()
+            got = z_rows(d, k + 1)
+            total = part[1, j, own_rows(got)] + z_got[d, k, got].astype(F32)
+            z_buf[d, k - 1, got] = total.astype(BF)
+        z_copy(d, k).start()
+
+    sum_out = remote(
+        fsum.at[pl.ds(pl.multiple_of(oc * 64, 64), 64)], fgot.at[core], f_send.at[3], f_recv.at[3], sib
+    )
+
+    def z_last():
+        y_add(0)
+        fsum[...] = part[1, 0, own_rows(slice(0, 128))]
+        for d in range(2):
+            z_copy(d, 1).wait_recv()
+            got = z_rows(d, 1)
+            fsum[got] += z_got[d, 0, got].astype(F32)
+        sum_out.start()
+        fgot[core] = fsum[pl.ds(pl.multiple_of(core * 64, 64), 64), :]
+
+    def z_finish():
+        sum_out.wait_recv()
+        for kk in range(2):
+            pool_out(1, kk, fgot[kk])
 
     def dq_tiles(h):
         for side in range(2):
@@ -363,73 +430,85 @@
             pltpu.make_async_copy(dq_st.at[core, :, lanes], dst, out_sem.at[2 + h]),
         ]
 
-    for cp in cot_out[0]:
-        cp.wait_recv()
-    for side in range(2):
-        cot_tiles(0, side)
-    own_part(0)
-    first = zs - 3
-
-    def pass0(i, carry):
-        late = jnp.minimum(lax.div(i, first), 1)
-        j = (1 - late) * i + late * (first + lax.rem(i - first + 2 + 3 * zs, 3))
-
-        @pl.when(i == first - 1)
-        def _():
-            for h in range(2):
-                gather_pass(h, hops - 1)
-
-        @pl.when(i == first)
-        def _():
-            gather_pass(0, hops)
-
-        unit(0, j)
-
-        @pl.when(i == first)
-        def _():
-            for d in range(2):
-                rs_stage(0, d, hops)
-
-        for d in range(2):
-            @pl.when(i == zs - 1 - d)
-            def _(d=d):
-                rs_stage(0, d, hops - 1)
-
+    near = zs - 3
+    cot_wait(0)
+    cot_tiles(0, 0)
+
+    def near_first(j, carry):
+        if hops > 3:
+            @pl.when(j == 3)
+            def _():
+                gather_pass(0, 2)
+
+        unit(0, j, 0)
         return carry
 
-    lax.fori_loop(0, zs, pass0, 0)
-
-    gather_pass(1, hops)
-    for cp in cot_out[1]:
-        cp.wait_recv()
-    for side in range(2):
-        cot_tiles(1, side)
-
-    def pass1(i, carry):
-        unit(1, zs - 1 - i)
+    def near_second(j, carry):
+        unit(0, j, 1)
+        return carry
+
+    def far(i, carry):
+        unit(0, near + lax.rem(i + 2, 3))
 
         @pl.when(i == 0)
         def _():
             for d in range(2):
-                rs_stage(1, d, hops)
-
-        for k in range(hops - 1, 0, -1):
+                rs_stage(d, hops)
+
+        return carry
+
+    lax.fori_loop(0, near, near_first, 0)
+    if hops > 3:
+        gather_pass(1, 2)
+    cot_next(1)
+    cot_wait(1)
+    cot_tiles(0, 1)
+    lax.fori_loop(0, near, near_second, 0)
+    own_part(0)
+    for h in range(2):
+        gather_pass(h, hops - 1)
+    cot_next(2)
+    gather_pass(0, hops)
+    lax.fori_loop(0, 3, far, 0)
+    for d in range(2):
+        rs_stage(d, hops - 1)
+    dq_tiles(0)
+    for cp in dq_copies(0):
+        cp.start()
+
+    gather_pass(1, hops)
+    for q in range(2):
+        cot_wait(2 + q)
+        cot_tiles(1, q)
+
+    def pass1(i, carry):
+        unit(1, zs - 1 - i)
+        y_start(zs - 1 - i)
+
+        @pl.when(i == 2)
+        def _():
             for d in range(2):
-                @pl.when(i == 2 * (hops - k) - 1 + d)
-                def _(d=d, k=k):
-                    rs_stage(1, d, k)
-
-            if k < hops - 1:
-                @pl.when(i == 2 * (hops - 1 - k))
-                def _(k=k):
-                    for d in range(2):
-                        rs_stage(0, d, k)
+                z_stage(d, hops)
+            for d in range(2):
+                if hops > 2:
+                    rs_stage(d, hops - 2)
+
+        for k in range(hops - 1, 1, -1):
+            @pl.when(i == 2 * (hops - k) + 2)
+            def _(k=k):
+                for d in range(2):
+                    z_stage(d, k)
+
+        if hops > 3:
+            @pl.when(i == zs - 3)
+            def _():
+                for d in range(2):
+                    rs_stage(d, hops - 3)
 
         return carry
 
     lax.fori_loop(0, zs, pass1, 0)
 
-    rs_last(0)
     own_part(1)
     ok_out = []
     for j, out in enumerate((dok_out, dov_out)):
@@ -439,24 +518,28 @@
         ok_out.append(pltpu.make_async_copy(ok_st.at[core, :, lanes], dst, out_sem.at[j]))
     for cp in ok_out:
         cp.start()
-    for h in range(2):
-        dq_tiles(h)
-        for cp in dq_copies(h):
-            cp.start()
-    rs_last(1)
-    f_finish(0)
+    rs_last()
+    for d in range(2):
+        z_stage(d, 1)
+    dq_tiles(1)
+    for cp in dq_copies(1):
+        cp.start()
+    rs_finish()
+    z_last()
     for cp in ok_out + dq_copies(0) + dq_copies(1):
         cp.wait()
-    for cp in kv_out[0] + kv_out[1] + cot_out[1] + sib_out + f_out[0]:
+    for cp in kv_out[0] + kv_out[1] + cot_out[3] + sib_out + f_out:
         cp.wait_send()
-    for h in range(2):
-        for d in range(2):
-            for t in range(1, hops + 1):
+    for d in range(2):
+        for t in range(1, hops + 1):
+            for h in range(2):
                 gather(h, d, t).wait_send()
-                rs_copy(h, d, t).wait_send()
-    f_finish(1)
-    for cp in f_out[1]:
-        cp.wait_send()
+            rs_copy(d, t).wait_send()
+            z_copy(d, t).wait_send()
+    for j in range(zs):
+        y_copy(j).wait_send()
+    z_finish()
+    sum_out.wait_send()
 
 
 def hand_over(*refs):
@@ -497,19 +580,26 @@
             pltpu.VMEM((256, 2048), BF),
             pltpu.VMEM((256, 2048), BF),
             pltpu.VMEM((2, zs, 256, 256), F32),
-            pltpu.VMEM((2, 2, hops, 256, 256), BF),
-            pltpu.VMEM((2, 2, hops, 256, 256), BF),
-            pltpu.VMEM((2, 256, 256), BF),
-            pltpu.VMEM((2, 4, 64, 256), BF),
+            pltpu.VMEM((2, hops, 256, 256), BF),
+            pltpu.VMEM((2, hops, 256, 256), BF),
+            pltpu.VMEM((zs, 128, 256), BF),
+            pltpu.VMEM((zs, 128, 256), BF),
+            pltpu.VMEM((2, hops, 128, 256), BF),
+            pltpu.VMEM((2, hops, 128, 256), BF),
+            pltpu.VMEM((256, 256), BF),
+            pltpu.VMEM((4, 64, 256), BF),
+            pltpu.VMEM((128, 256), F32),
+            pltpu.VMEM((2, 64, 256), F32),
             pltpu.VMEM((2, 128, 2048), BF),
             pltpu.VMEM((2, 128, 512), BF),
             pltpu.VMEM((32, 128), F32),
             pltpu.VMEM((2, 16, 128), F32),
             pltpu.VMEM((blocks, 128), F32),
             pltpu.VMEM((2, blocks, 128), F32),
-            dma((8,)), dma((6,)), dma((6,)), dma((2, 2)), dma((2, 2)), dma((3, 2, 2)), dma((3, 2, 2)),
-            dma((2, 2, hops)), dma((2, 2, hops)), dma((2, 2, hops)), dma((2, 2, hops)),
-            dma((2, 3)), dma((2, 3)), dma((4,)), dma((4,)), dma((4,)),
+            dma((8,)), dma((6,)), dma((6,)), dma((4, 2)), dma((4, 2)), dma((3, 2, 2)), dma((3, 2, 2)),
+            dma((2, 2, hops)), dma((2, 2, hops)), dma((2, hops)), dma((2, hops)),
+            dma((zs,)), dma((zs,)), dma((2, hops)), dma((2, hops)),
+            dma((4,)), dma((4,)), dma((4,)), dma((4,)), dma((4,)),
         ],
         compiler_params=pltpu.CompilerParams(
             collective_id=0, has_side_effects=True, vmem_limit_bytes=56 * 1024 * 1024

time: 79.2 us -> 72.5 us (0.915); the launches traced: 78.2 us -> 72.3 us
  Pallas kernels: 77.5 us -> 71.7 us
    pallas_call x1, Pallas kernels: 75 us -> 69.1 us  [local(): pl.pallas_call(functools.partial(kernel, zs, pipes), out_shape=(jax.Shape...]
where the time goes in v3:
time: 72.5 us; the launch traced here: 72.3 us
  Pallas kernels  71.7 us (99%)
    pallas_call x1, Pallas kernels, local(): pl.pallas_call(functools.partial(kernel, zs, pipes), out_shape=(jax.Shape...  69.1 us
    pallas_call x1, Pallas kernels, local(): pl.pallas_call(hand_over, out_shape=tuple((jax.ShapeDtypeStruct(out.shape...  2.53 us

profile of v3, /device:TPU:1, one launch (start us, length us, event | category | flops | bytes accessed | tf_op | source)
XLA Modules:
  0.0 72.3 jit_solution(9897461661439518661)
XLA Ops:
  0.6 69.1 %shard_map.137 = (bf16[128,4096]{1,0:T(8,128)(2,1)}, bf16[128,512]{1,0:T(8,128)(2,1)}, bf16[128,512]{1,0:T(8,128)(2,1)}, f32[64,512]{1,0:T(8,128)}, f32[64,512]{1,0:T(8,128)}) custom-call(bf16[128,4096]{1,0:T(8,128)(2,1)} %bitcast.16, bf16[128,4096]{1,0:T(8,128)(2,1)} %bitcast.17, bf16[128,4096]{1,0:T(8,128)(2,1)} %bitcast.18, f32[32,128]{1,0:T(8,128)} %bitcast.23, ...), custom_call_target="tpu_custom_call" | custom-call | tf_op jit(solution)/shard_map/pallas_call | solution.py:557
  69.8 2.5 %shard_map.138 = (bf16[128,4096]{1,0:T(8,128)(2,1)}, bf16[128,512]{1,0:T(8,128)(2,1)}, bf16[128,512]{1,0:T(8,128)(2,1)}, f32[64,512]{1,0:T(8,128)}, f32[64,512]{1,0:T(8,128)}) custom-call(bf16[128,4096]{1,0:T(8,128)(2,1)} %get-tuple-element.15.refs_0_, bf16[128,512]{1,0:T(8,128)(2,1)} %get-tuple-element.16.refs_1_, ...), custom_call_target="tpu_custom_call" | custom-call | tf_op jit(solution)/shard_map/pallas_call | solution.py:608

commit v4 on v3

--- a/solution.py
+++ b/solution.py
@@ -69,6 +69,17 @@
 
     my_rows = pl.ds(pl.multiple_of(core * ROWS, ROWS), ROWS)
     my_keys = pl.ds(pl.multiple_of(yl * 128 + core * 64, 64), 64)
+
+    barrier = pltpu.get_barrier_semaphore()
+    partners = [
+        sib,
+        dev(p, 1 - yl, z, 0), dev(p, 1 - yl, z, 1),
+        ring_dst[0], ring_dst[1],
+        dev(p_dn, yl, z, 0), dev(p_dn, yl, z, 1),
+        dev(p_up, yl, z, 0), dev(p_up, yl, z, 1),
+    ]
+    for to in partners:
+        pl.semaphore_signal(barrier, inc=1, device_id=to, device_id_type=MESH)
 
     loc = [
         pltpu.make_async_copy(lanes_at(q_hbm, core * 2048, 2048), qb.at[my_rows], loc_sem.at[0]),
@@ -105,16 +116,6 @@
     bp[core] = offs
     ln_r[core] = ln_t[pl.ds(pl.multiple_of(core * 16, 16), 16), :]
 
-    barrier = pltpu.get_barrier_semaphore()
-    partners = [
-        sib,
-        dev(p, 1 - yl, z, 0), dev(p, 1 - yl, z, 1),
-        ring_dst[0], ring_dst[1],
-        dev(p_dn, yl, z, 0), dev(p_dn, yl, z, 1),
-        dev(p_up, yl, z, 0), dev(p_up, yl, z, 1),
-    ]
-    for to in partners:
-        pl.semaphore_signal(barrier, inc=1, device_id=to, device_id_type=MESH)
     pl.semaphore_wait(barrier, len(partners))
 
     group = [(yl, oc), (1 - yl, core), (1 - yl, oc)]
@@ -156,12 +157,6 @@
         for part_i in range(4)
     ]
 
-    def cot_next(done):
-        for cp in cot_out[done]:
-            cp.wait_send()
-        for cp in cot_out[done + 1]:
-            cp.start()
-
     def cot_wait(i):
         for cp in cot_out[i]:
             cp.wait_recv()
@@ -191,8 +186,9 @@
             cp.wait_recv()
         for d in range(2):
             gather(h, d, 1).start()
-    for cp in cot_out[0]:
-        cp.start()
+    for i in range(4):
+        for cp in cot_out[i]:
+            cp.start()
 
     qt[:, 128:256, :] = jnp.zeros((2, 128, 2048), BF)
     ct[:, 128:256, :] = jnp.zeros((2, 128, 2048), BF)
@@ -245,7 +241,6 @@
         gather_pass(0, 1)
     for side in range(2):
         query_tiles(1, side)
-    cot_next(0)
     if hops > 2:
         gather_pass(1, 1)
 
@@ -281,13 +276,15 @@
             ok_st[side, :, h * 128 : (h + 1) * 128] = (dk * SCALE).astype(BF)
             ok_st[side, :, 256 + h * 128 : 256 + (h + 1) * 128] = dv.astype(BF)
 
-    def unit(h, j, q=None):
+    def unit(h, k, q=None):
         lo, hi = (0, 2048) if q is None else (q * 1024, (q + 1) * 1024)
-        offset = lax.div(j + 1, 2) * (1 - 2 * lax.rem(j, 2))
-        chunk = lax.rem(z + zs + offset, zs)
-        k_l = kv[h, chunk, :, 0:128]
-        k_full = jnp.concatenate([k_l, kaug[chunk]], 1)
-        v_full = jnp.concatenate([kv[h, chunk, :, 128:256], v_cst], 1)
+        above = lax.rem(2 * k, zs)
+        places = (2 * k - 1, above)
+        ids = (lax.rem(z + zs - k, zs), lax.rem(z + lax.div(above, 2), zs))
+        k_l = jnp.concatenate([kv[h, i, :, 0:128] for i in ids], 0)
+        v_l = jnp.concatenate([kv[h, i, :, 128:256] for i in ids], 0)
+        k_full = jnp.concatenate([k_l, jnp.concatenate([kaug[i] for i in ids], 0)], 1)
+        v_full = jnp.concatenate([v_l, jnp.concatenate([v_cst, v_cst], 0)], 1)
         for n in range(lo, hi, 512):
             cols = slice(n, n + 512)
             pr = jnp.exp2(dot(k_full, qt[h, :, cols]) * EXP_SCALE)
@@ -297,12 +294,14 @@
         dqt[h, :, lo:hi] += dot(k_l.T, ds_s[:, lo:hi])
         dk = dot(ds_s[:, lo:hi], qh[h, lo:hi])
         dv = dot(p_s[:, lo:hi], ch[h, lo:hi])
-        if q == 1:
-            part[h, j, :, 0:128] += dk
-            part[h, j, :, 128:256] += dv
-        else:
-            part[h, j, :, 0:128] = dk
-            part[h, j, :, 128:256] = dv
+        for i, j in enumerate(places):
+            keys = slice(i * 256, (i + 1) * 256)
+            if q == 1:
+                part[h, j, :, 0:128] += dk[keys]
+                part[h, j, :, 128:256] += dv[keys]
+            else:
+                part[h, j, :, 0:128] = dk[keys]
+                part[h, j, :, 128:256] = dv[keys]
 
     def rs_rows(d, k):
         return slice(0, 256) if k < hops else slice(d * 128, (d + 1) * 128)
@@ -430,84 +429,96 @@
             pltpu.make_async_copy(dq_st.at[core, :, lanes], dst, out_sem.at[2 + h]),
         ]
 
-    near = zs - 3
+    near = hops - 2
     cot_wait(0)
     cot_tiles(0, 0)
 
-    def near_first(j, carry):
-        if hops > 3:
-            @pl.when(j == 3)
+    def near_first(i, carry):
+        if near > 1:
+            @pl.when(i == 1)
             def _():
                 gather_pass(0, 2)
 
-        unit(0, j, 0)
+        unit(0, i + 1, 0)
         return carry
 
-    def near_second(j, carry):
-        unit(0, j, 1)
+    def near_second(i, carry):
+        unit(0, i + 1, 1)
         return carry
 
     def far(i, carry):
-        unit(0, near + lax.rem(i + 2, 3))
+        @pl.when(i == 1)
+        def _():
+            gather_pass(1, hops - 1)
+            gather_pass(0, hops)
+
+        unit(0, hops - 1 + i)
+        return carry
+
+    if near > 0:
+        lax.fori_loop(0, near, near_first, 0)
+    if near > 1:
+        gather_pass(1, 2)
+    cot_wait(1)
+    cot_tiles(0, 1)
+    if near > 0:
+        lax.fori_loop(0, near, near_second, 0)
+    own_part(0)
+    gather_pass(0, hops - 1)
+    lax.fori_loop(0, 2, far, 0)
+    for d in range(2):
+        rs_stage(d, hops)
+
+    gather_pass(1, hops)
+    cot_wait(2)
+    cot_tiles(1, 0)
+
+    def far_first(i, carry):
+        unit(1, hops - i, 0)
 
         @pl.when(i == 0)
         def _():
             for d in range(2):
-                rs_stage(d, hops)
+                rs_stage(d, hops - 1)
 
         return carry
 
-    lax.fori_loop(0, near, near_first, 0)
-    if hops > 3:
-        gather_pass(1, 2)
-    cot_next(1)
-    cot_wait(1)
-    cot_tiles(0, 1)
-    lax.fori_loop(0, near, near_second, 0)
-    own_part(0)
-    for h in range(2):
-        gather_pass(h, hops - 1)
-    cot_next(2)
-    gather_pass(0, hops)
-    lax.fori_loop(0, 3, far, 0)
-    for d in range(2):
-        rs_stage(d, hops - 1)
-    dq_tiles(0)
-    for cp in dq_copies(0):
-        cp.start()
-
-    gather_pass(1, hops)
-    for q in range(2):
-        cot_wait(2 + q)
-        cot_tiles(1, q)
-
-    def pass1(i, carry):
-        unit(1, zs - 1 - i)
-        y_start(zs - 1 - i)
-
-        @pl.when(i == 2)
+    def far_second(i, carry):
+        unit(1, hops - i, 1)
+        y_start(2 * (hops - i) - 1)
+
+        @pl.when(i == 1)
         def _():
-            for d in range(2):
-                z_stage(d, hops)
-            for d in range(2):
-                if hops > 2:
+            y_start(2 * (hops - 1))
+            if hops > 2:
+                for d in range(2):
                     rs_stage(d, hops - 2)
 
-        for k in range(hops - 1, 1, -1):
-            @pl.when(i == 2 * (hops - k) + 2)
-            def _(k=k):
+        return carry
+
+    def near_both(i, carry):
+        k = near - i
+        unit(1, k)
+        y_start(2 * k - 1)
+        y_start(2 * k)
+        for n in range(2):
+            @pl.when(i == n)
+            def _(n=n):
                 for d in range(2):
-                    z_stage(d, k)
-
-        if hops > 3:
-            @pl.when(i == zs - 3)
-            def _():
-                for d in range(2):
-                    rs_stage(d, hops - 3)
+                    z_stage(d, hops - n)
+                if n == 1:
+                    for d in range(2):
+                        rs_stage(d, hops - 3)
 
         return carry
 
-    lax.fori_loop(0, zs, pass1, 0)
+    lax.fori_loop(0, 2, far_first, 0)
+    cot_wait(3)
+    cot_tiles(1, 1)
+    lax.fori_loop(0, 2, far_second, 0)
+    if near > 0:
+        lax.fori_loop(0, near, near_both, 0)
+    y_start(0)
 
     own_part(1)
     ok_out = []
@@ -518,17 +529,19 @@
         ok_out.append(pltpu.make_async_copy(ok_st.at[core, :, lanes], dst, out_sem.at[j]))
     for cp in ok_out:
         cp.start()
-    rs_last()
-    for d in range(2):
-        z_stage(d, 1)
-    dq_tiles(1)
-    for cp in dq_copies(1):
-        cp.start()
+    for k in (2, 1):
+        dq_tiles(2 - k)
+        for cp in dq_copies(2 - k):
+            cp.start()
+        for d in range(2):
+            z_stage(d, k)
+        if k == 2:
+            rs_last()
     rs_finish()
     z_last()
     for cp in ok_out + dq_copies(0) + dq_copies(1):
         cp.wait()
-    for cp in kv_out[0] + kv_out[1] + cot_out[3] + sib_out + f_out:
+    for cp in kv_out[0] + kv_out[1] + sum(cot_out, []) + sib_out + f_out:
         cp.wait_send()
     for d in range(2):
         for t in range(1, hops + 1):
@@ -577,8 +590,8 @@
             pltpu.VMEM((zs, 256, 128), BF),
             pltpu.VMEM((256, 512), BF),
             pltpu.VMEM((2, 128, 2048), F32),
-            pltpu.VMEM((256, 2048), BF),
-            pltpu.VMEM((256, 2048), BF),
+            pltpu.VMEM((512, 2048), BF),
+            pltpu.VMEM((512, 2048), BF),
             pltpu.VMEM((2, zs, 256, 256), F32),
             pltpu.VMEM((2, hops, 256, 256), BF),
             pltpu.VMEM((2, hops, 256, 256), BF),
@@ -605,11 +618,13 @@
             collective_id=0, has_side_effects=True, vmem_limit_bytes=56 * 1024 * 1024
         ),
     )(q[0], o[0], g[0], ln[0].T, ok[0], ov[0], pk[0], pv[0], tab[0], lens)
+    halves = [pl.BlockSpec((out.shape[0] // 2, out.shape[1]), lambda i: (i, 0)) for out in outs]
     outs = pl.pallas_call(
         hand_over,
         out_shape=tuple(jax.ShapeDtypeStruct(out.shape, out.dtype) for out in outs),
-        in_specs=[vmem] * 5,
-        out_specs=(vmem,) * 5,
+        grid=(2,),
+        in_specs=halves,
+        out_specs=tuple(halves),
     )(*outs)
     return tuple(out[None] for out in outs)
 

time: 72.5 us -> 72.3 us (level)
  no operation moved by 1% of the time
where the time goes in v4:
time: 72.3 us; the launch traced here: 72.1 us
  Pallas kernels  71.3 us (99%)
  between operations  0.78 us (1%)
    pallas_call x1, Pallas kernels, local(): pl.pallas_call(functools.partial(kernel, zs, pipes), out_shape=(jax.Shape...  69 us
    pallas_call x1, Pallas kernels, local(): pl.pallas_call(hand_over, out_shape=tuple((jax.ShapeDtypeStruct(out.shape...  2.32 us

profile of v4, /device:TPU:1, one launch (start us, length us, event | category | flops | bytes accessed | tf_op | source)
XLA Modules:
  0.0 72.1 jit_solution(2204443467250524899)
XLA Ops:
  0.6 69.0 %shard_map.137 = (bf16[128,4096]{1,0:T(8,128)(2,1)}, bf16[128,512]{1,0:T(8,128)(2,1)}, bf16[128,512]{1,0:T(8,128)(2,1)}, f32[64,512]{1,0:T(8,128)}, f32[64,512]{1,0:T(8,128)}) custom-call(bf16[128,4096]{1,0:T(8,128)(2,1)} %bitcast.16, bf16[128,4096]{1,0:T(8,128)(2,1)} %bitcast.17, bf16[128,4096]{1,0:T(8,128)(2,1)} %bitcast.18, f32[32,128]{1,0:T(8,128)} %bitcast.23, ...), custom_call_target="tpu_custom_call" | custom-call | tf_op jit(solution)/shard_map/pallas_call | solution.py:570
  69.6 2.3 %shard_map.138 = (bf16[128,4096]{1,0:T(8,128)(2,1)}, bf16[128,512]{1,0:T(8,128)(2,1)}, bf16[128,512]{1,0:T(8,128)(2,1)}, f32[64,512]{1,0:T(8,128)}, f32[64,512]{1,0:T(8,128)}) custom-call(bf16[128,4096]{1,0:T(8,128)(2,1)} %get-tuple-element.15.refs_0_, bf16[128,512]{1,0:T(8,128)(2,1)} %get-tuple-element.16.refs_1_, ...), custom_call_target="tpu_custom_call" | custom-call | tf_op jit(solution)/shard_map/pallas_call | solution.py:622

commit v5 on v4

--- a/solution.py
+++ b/solution.py
@@ -487,12 +487,15 @@
         unit(1, hops - i, 1)
         y_start(2 * (hops - i) - 1)
 
+        @pl.when(i == 0)
+        def _():
+            if hops > 2:
+                for d in range(2):
+                    rs_stage(d, hops - 2)
+
         @pl.when(i == 1)
         def _():
             y_start(2 * (hops - 1))
-            if hops > 2:
-                for d in range(2):
-                    rs_stage(d, hops - 2)
 
         return carry
 
@@ -501,12 +504,12 @@
         unit(1, k)
         y_start(2 * k - 1)
         y_start(2 * k)
-        for n in range(2):
+        for n in range(near):
             @pl.when(i == n)
             def _(n=n):
                 for d in range(2):
-                    z_stage(d, hops - n)
-                if n == 1:
+                    z_stage(d, hops - 1 - n)
+                if n == 0 and hops > 3:
                     for d in range(2):
                         rs_stage(d, hops - 3)
 
@@ -516,6 +519,8 @@
     cot_wait(3)
     cot_tiles(1, 1)
     lax.fori_loop(0, 2, far_second, 0)
+    for d in range(2):
+        z_stage(d, hops)
     if near > 0:
         lax.fori_loop(0, near, near_both, 0)
     y_start(0)
@@ -529,14 +534,13 @@
         ok_out.append(pltpu.make_async_copy(ok_st.at[core, :, lanes], dst, out_sem.at[j]))
     for cp in ok_out:
         cp.start()
-    for k in (2, 1):
-        dq_tiles(2 - k)
-        for cp in dq_copies(2 - k):
+    for h in range(2):
+        dq_tiles(h)
+        for cp in dq_copies(h):
             cp.start()
-        for d in range(2):
-            z_stage(d, k)
-        if k == 2:
-            rs_last()
+    for d in range(2):
+        z_stage(d, 1)
+    rs_last()
     rs_finish()
     z_last()
     for cp in ok_out + dq_copies(0) + dq_copies(1):

time: 72.3 us -> 73.5 us (1.017)
  Pallas kernels: 71.3 us -> 72.7 us
    pallas_call x1, Pallas kernels: 69 us -> 70.4 us  [local(): pl.pallas_call(functools.partial(kernel, zs, pipes), out_shape=(jax.Shape...]
where the time goes in v5:
time: 73.5 us; the launch traced here: 73.3 us
  Pallas kernels  72.7 us (99%)
    pallas_call x1, Pallas kernels, local(): pl.pallas_call(functools.partial(kernel, zs, pipes), out_shape=(jax.Shape...  70.4 us
    pallas_call x1, Pallas kernels, local(): pl.pallas_call(hand_over, out_shape=tuple((jax.ShapeDtypeStruct(out.shape...  2.32 us

profile of v5, /device:TPU:1, one launch (start us, length us, event | category | flops | bytes accessed | tf_op | source)
XLA Modules:
  0.0 73.3 jit_solution(12424885402836413783)
XLA Ops:
  0.6 70.4 %shard_map.137 = (bf16[128,4096]{1,0:T(8,128)(2,1)}, bf16[128,512]{1,0:T(8,128)(2,1)}, bf16[128,512]{1,0:T(8,128)(2,1)}, f32[64,512]{1,0:T(8,128)}, f32[64,512]{1,0:T(8,128)}) custom-call(bf16[128,4096]{1,0:T(8,128)(2,1)} %bitcast.16, bf16[128,4096]{1,0:T(8,128)(2,1)} %bitcast.17, bf16[128,4096]{1,0:T(8,128)(2,1)} %bitcast.18, f32[32,128]{1,0:T(8,128)} %bitcast.23, ...), custom_call_target="tpu_custom_call" | custom-call | tf_op jit(solution)/shard_map/pallas_call | solution.py:574
  71.0 2.3 %shard_map.138 = (bf16[128,4096]{1,0:T(8,128)(2,1)}, bf16[128,512]{1,0:T(8,128)(2,1)}, bf16[128,512]{1,0:T(8,128)(2,1)}, f32[64,512]{1,0:T(8,128)}, f32[64,512]{1,0:T(8,128)}) custom-call(bf16[128,4096]{1,0:T(8,128)(2,1)} %get-tuple-element.15.refs_0_, bf16[128,512]{1,0:T(8,128)(2,1)} %get-tuple-element.16.refs_1_, ...), custom_call_target="tpu_custom_call" | custom-call | tf_op jit(solution)/shard_map/pallas_call | solution.py:626
